TPU v7x, 512 devices: a whole 4x8x8 slice. The times are simulated.
512 devices in a mesh: replica: 64 (over z, x, core), tensor: 8 (over y).
Axes of the slice: x: 4, y: 8, z: 8, core: 2. Of those that a mesh axis runs over, the one named last changes fastest.
Arguments:
- tokens: bfloat16 [1024, 4, 8192], P('replica', None, 'tensor'), may hold values from -6 to 6
- value_matrix: bfloat16 [8192, 1024], P(None, 'tensor'), may hold values from -0.0625 to 0.0625
- queries: bfloat16 [1024, 4, 8192], P('replica', None, 'tensor'), may hold values from -400 to 400, as said below
- draft_keys: bfloat16 [1024, 4, 1024], P('replica', None, 'tensor'), may hold values from -6 to 6
- key_cache_before: bfloat16 [1024, 64, 1024], P('replica', None, 'tensor'), may hold values from -6 to 6
- value_cache_before: bfloat16 [1024, 64, 1024], P('replica', None, 'tensor'), may hold values from -6 to 6
- cache_length: int32 [1024], P('replica'), may hold values from 1 to 60, as said below
- migrations: int32 [64, 3, 3], P('replica'), may hold values from 0 to 63, as said below
- block_adapter_index: int32 [64, 4], P('replica'), may hold values from 0 to 63, as said below
- adapter_replica: int32 [64], replicated, may hold values from 0 to 63, as said below
- adapter_shrink: bfloat16 [64, 8192, 64], P('replica', 'tensor'), may hold values from -0.0625 to 0.0625
- adapter_expand: bfloat16 [64, 64, 1024], P('replica', None, 'tensor'), may hold values from -0.75 to 0.75
Outputs:
- attended: bfloat16 [1024, 4, 8192], P('replica', None, 'tensor')
- keys_out: bfloat16 [1024, 64, 1024], P('replica', None, 'tensor')
- values_out: bfloat16 [1024, 64, 1024], P('replica', None, 'tensor')
Inputs may be any that keep to these rules, and one draw needn't show every extreme that they name: `queries`: each draft token's query features; their scale may differ from head to head. `cache_length`: every request has room for its 4 draft tokens. `migrations`: row q lists the 3 requests leaving replica q as (slot on q, destination replica, slot on the destination), at distinct slots of q. Every replica uses the same 3 distinct nonzero offsets from source to destination, counted round the replicas; one of them is 1 and one is half the number of replicas. So every replica sends and receives exactly 3 requests, at most one to or from each peer, and each slot it gives up receives exactly one arriving request. `block_adapter_index`: adapter ids of the blocks; some adapters are used by many blocks. `adapter_replica`: each replica holds exactly one adapter.
All inputs are finite; a program needn't handle non-finite values.
Results may differ from a plain program's by a relative error of at most 0.0054.
Values may be sent and summed in bfloat16 or wider, within the bound.
A program may use at most 64 MiB of HBM per device.

v0:
```python
import math

import jax
import jax.numpy as jnp
from jax import lax
from jax.sharding import PartitionSpec as P

HD = 128


def owners_of(block_ids, adapter_replica):
    catalog = jnp.arange(adapter_replica.shape[0], dtype=jnp.int32)
    matches = block_ids[..., None] == catalog
    return jnp.sum(jnp.where(matches, adapter_replica, 0), axis=-1)


def selector(stored_at, count):
    indices = jnp.arange(count, dtype=jnp.int32)
    return (stored_at[:, None] == indices[None, :]).astype(jnp.bfloat16)


def body(
    tokens,
    value_matrix,
    queries,
    draft_keys,
    key_cache_before,
    value_cache_before,
    cache_length,
    migrations,
    block_adapter_index,
    adapter_replica,
    adapter_shrink,
    adapter_expand,
):
    slots, steps, width_part = tokens.shape
    head_cols = value_matrix.shape[1]
    blocks = block_adapter_index.shape[1]
    block_rows = slots * steps // blocks
    token_rows = tokens.reshape(slots * steps, width_part)
    base = jnp.dot(
        lax.all_gather(token_rows, "tensor", axis=1, tiled=True),
        value_matrix,
        preferred_element_type=jnp.float32,
    )
    replica_id = lax.axis_index("replica")
    stored_at = owners_of(block_adapter_index[0], adapter_replica)
    whole_down, whole_up = (
        lax.all_gather(adapter_shrink, "replica", axis=0, tiled=True),
        lax.all_gather(adapter_expand, "replica", axis=0, tiled=True),
    )
    chosen = selector(stored_at, whole_down.shape[0])
    down_chosen = jnp.einsum(
        "bk,kdr->bdr", chosen, whole_down, preferred_element_type=jnp.float32
    ).astype(jnp.bfloat16)
    up_chosen = jnp.einsum(
        "bk,krc->brc", chosen, whole_up, preferred_element_type=jnp.float32
    ).astype(jnp.bfloat16)
    grouped = token_rows.reshape(blocks, block_rows, width_part)
    partial_value = jnp.einsum(
        "bnd,bdr->bnr", grouped, down_chosen, preferred_element_type=jnp.float32
    )
    shrink = lax.psum(partial_value, "tensor").astype(jnp.bfloat16)
    delta = jnp.einsum(
        "bnr,brc->bnc", shrink, up_chosen, preferred_element_type=jnp.float32
    ).reshape(slots * steps, head_cols)
    fresh_values = (base + delta).astype(jnp.bfloat16).reshape(slots, steps, head_cols)
    leaving = migrations[0]
    out_keys = jnp.take(key_cache_before, leaving[:, 0], axis=0)
    out_values = jnp.take(value_cache_before, leaving[:, 0], axis=0)
    out_filled = jnp.take(cache_length, leaving[:, 0], axis=0)
    slot_ids = jnp.arange(slots, dtype=jnp.int32)
    all_keys, all_values, all_route, all_filled = (
        lax.all_gather(out_keys, "replica", axis=0, tiled=True),
        lax.all_gather(out_values, "replica", axis=0, tiled=True),
        lax.all_gather(leaving[:, 1:3], "replica", axis=0, tiled=True),
        lax.all_gather(out_filled, "replica", axis=0, tiled=True),
    )
    matches = (all_route[:, 0:1] == replica_id) & (all_route[:, 1:2] == slot_ids[None, :])
    arrived = jnp.sum(jnp.where(matches, all_filled[:, None], 0), axis=0).astype(jnp.int32)
    landed = jnp.any(matches, axis=0)
    weight = matches.astype(jnp.bfloat16)
    placed_keys = jnp.einsum(
        "ms,mlc->slc", weight, all_keys, preferred_element_type=jnp.float32
    ).astype(jnp.bfloat16)
    placed_values = jnp.einsum(
        "ms,mlc->slc", weight, all_values, preferred_element_type=jnp.float32
    ).astype(jnp.bfloat16)
    held_keys = jnp.where(landed[:, None, None], placed_keys, key_cache_before)
    held_values = jnp.where(landed[:, None, None], placed_values, value_cache_before)
    held_filled = jnp.where(landed, arrived, cache_length)
    places = jnp.arange(held_keys.shape[1], dtype=jnp.int32)
    step_ids = jnp.arange(steps, dtype=jnp.int32)
    token_position = held_filled[:, None] + step_ids[None, :]
    writes = places[None, :, None] == token_position[:, None, :]
    written = jnp.any(writes, axis=2)[:, :, None]
    write_weight = writes.astype(jnp.bfloat16)
    keys_out = jnp.where(
        written,
        jnp.einsum(
            "sln,snc->slc", write_weight, draft_keys, preferred_element_type=jnp.float32
        ).astype(jnp.bfloat16),
        held_keys,
    )
    values_out = jnp.where(
        written,
        jnp.einsum(
            "sln,snc->slc", write_weight, fresh_values, preferred_element_type=jnp.float32
        ).astype(jnp.bfloat16),
        held_values,
    )
    kv_heads = head_cols // HD
    query_heads = queries.shape[2] // HD
    group = query_heads // kv_heads
    shaped_q = queries.reshape(slots, steps, kv_heads, group, HD)
    shaped_k = keys_out.reshape(slots, -1, kv_heads, HD)
    scores = jnp.einsum(
        "snkgd,slkd->snkgl", shaped_q, shaped_k, preferred_element_type=jnp.float32
    ) * (1.0 / math.sqrt(HD))
    allowed = (places[None, None, :] <= token_position[:, :, None])[:, :, None, None, :]
    masked = jnp.where(allowed, scores, -1e30)
    top = jnp.max(masked, axis=-1, keepdims=True)
    raised = jnp.where(allowed, jnp.exp(masked - top), 0.0)
    weights = (raised / jnp.sum(raised, axis=-1, keepdims=True)).astype(jnp.bfloat16)
    shaped_v = values_out.reshape(slots, -1, kv_heads, HD)
    attended = jnp.einsum(
        "snkgl,slkd->snkgd", weights, shaped_v, preferred_element_type=jnp.float32
    )
    return (
        attended.reshape(slots, steps, query_heads * HD).astype(jnp.bfloat16),
        keys_out,
        values_out,
    )


def solution(mesh):
    placed = (
        P("replica", None, "tensor"),
        P(None, "tensor"),
        P("replica", None, "tensor"),
        P("replica", None, "tensor"),
        P("replica", None, "tensor"),
        P("replica", None, "tensor"),
        P("replica"),
        P("replica", None, None),
        P("replica", None),
        P(),
        P("replica", "tensor", None),
        P("replica", None, "tensor"),
    )
    return jax.shard_map(
        body,
        mesh=mesh,
        in_specs=placed,
        out_specs=(
            P("replica", None, "tensor"),
            P("replica", None, "tensor"),
            P("replica", None, "tensor"),
        ),
        check_vma=False,
    )
```

profile of v0, /device:TPU:1, one launch (start us, length us, event | category | flops | bytes accessed | tf_op | source)
XLA Modules:
  0.0 406.1 jit_solution(11458312940798593351)
XLA Ops:
  7.2 0.7 all-gather.11.cloned.1.call-update
  7.9 0.0 all-gather.15.cloned.1.call-start
  8.0 0.7 copy.72
  8.6 0.1 fusion.44
  8.8 1.5 gather_fusion.2
  10.3 1.5 gather_fusion.1
  11.9 0.7 broadcast_select_fusion
  12.6 0.0 all-gather.13.cloned.1.call-start
  12.6 0.7 all-gather.13.cloned.1.call-update
  13.4 0.5 all-gather.9.cloned.1.call-update
  13.9 0.0 all-gather.7.cloned.1.call-start
  14.0 1.6 reshape.101
  15.6 0.9 reshape_reshape.3
  16.6 0.1 slice.14
  16.6 0.1 and_reduce_fusion
  16.8 0.1 copy.34
  16.9 51.1 %all-gather = s32[64,3,2]{1,2,0:T(2,128)S(1)} all-gather(s32[1,3,2]{1,2,0:T(2,128)S(1)} %bitcast.66), channel_id=1, replica_groups=mesh['replica'=64,'tensor'=8] {'replica'}, dimensions={0}, use_global_device_ids=true | all-gather | bytes 1560 | tf_op jit(solution)/shard_map/all_gather | solution.py:76
  68.0 0.1 reshape.136
  68.2 1.3 dynamic-slice
  70.1 1.3 gather_fusion
  71.4 0.1 select_dynamic-update-slice_fusion
  71.5 14.5 %all-reduce = s32[192]{0:T(256)S(1)} all-reduce(s32[192]{0:T(256)S(1)} %select_dynamic-update-slice_fusion), channel_id=1, replica_groups=mesh['replica'=64,'tensor'=8] {'replica'}, use_global_device_ids=true, to_apply=%add | all-reduce | flops 192 | bytes 1536
  86.0 0.1 fusion.34
  86.1 0.1 select_reduce_fusion
  86.2 0.7 select_n.53
  86.9 0.1 iota_add_fusion
  87.0 0.1 fusion.28
  87.1 0.1 iota_compare_fusion
  87.2 1.0 reshape.104
  88.1 0.9 select_reduce_fusion.1
  89.0 10.8 %all-gather.11.cloned.1.call-done = bf16[64,64,128]{2,1,0:T(8,128)(2,1)} async-done(((bf16[1,64,128]{2,1,0:T(8,128)(2,1)}), bf16[64,64,128]{2,1,0:T(8,128)(2,1)}) %all-gather.11.cloned.1.call-update) | async-done | bytes 1048592 | tf_op jit(solution)/shard_map/all_gather | solution.py:50
  99.8 1.9 convolution_convert_fusion.3
  101.7 83.9 %all-gather.15.cloned.1.call-done = bf16[192,64,128]{2,1,0:T(8,128)(2,1)} async-done(((bf16[3,64,128]{2,1,0:T(8,128)(2,1)}), bf16[192,64,128]{2,1,0:T(8,128)(2,1)}) %all-gather.15.cloned.1.call-update) | async-done | bytes 3145744 | tf_op jit(solution)/shard_map/all_gather | solution.py:74
  185.5 3.7 fusion.2
  189.2 0.5 fusion.11
  189.8 0.3 fusion.48
  190.1 0.3 fusion.21
  190.4 79.9 %all-gather.13.cloned.1.call-done = bf16[192,64,128]{2,1,0:T(8,128)(2,1)} async-done(((bf16[3,64,128]{2,1,0:T(8,128)(2,1)}), bf16[192,64,128]{2,1,0:T(8,128)(2,1)}) %all-gather.13.cloned.1.call-update) | async-done | bytes 3145744 | tf_op jit(solution)/shard_map/all_gather | solution.py:75
  270.3 3.7 fusion.4
  274.0 86.1 %all-gather.9.cloned.1.call-done = bf16[64,1024,64]{1,2,0:T(8,128)(2,1)} async-done(((bf16[1,1024,64]{1,2,0:T(8,128)(2,1)}), bf16[64,1024,64]{1,2,0:T(8,128)(2,1)}) %all-gather.9.cloned.1.call-update) | async-done | bytes 8388624 | tf_op jit(solution)/shard_map/all_gather | solution.py:49
  360.1 12.5 %fusion.6 = bf16[4,1024,64]{1,0,2:T(4,128)(2,1)S(1)} fusion(bf16[64,1024,64]{1,2,0:T(8,128)(2,1)} %all-gather.9.cloned.1.call-done, s32[4]{0:T(128)S(1)} %select_reduce_fusion.1), kind=kOutput, calls=%fused_computation.9 | convolution fusion | flops 33816832 | bytes 8912912 | tf_op jit(solution)/shard_map/bk,kdr->bdr/dot_general | solution.py:53
  372.6 0.3 convolution_bitcast_fusion
  372.9 23.2 %psum.7 = bf16[4,16,64]{2,1,0:T(8,128)(2,1)S(1)} all-reduce(f32[4,16,64]{2,1,0:T(8,128)S(1)} %convolution_bitcast_fusion), channel_id=1, replica_groups=mesh['replica'=64,'tensor'=8] {'tensor'}, use_global_device_ids=true, to_apply=%region_4.5 | all-reduce | flops 4096 | bytes 24576 | tf_op jit(solution)/shard_map/psum | solution.py:63
  396.1 0.1 fusion.26
  396.3 1.7 fusion.14
  398.0 0.5 fusion.10
  398.6 0.3 fusion.13
  398.9 0.7 convert_element_type.54
  (33 shorter events, 0.2 us)
Async XLA Ops:
  7.2 389.1 %copy-start = (bf16[8192,128]{1,0:T(8,128)(2,1)S(1)}, bf16[8192,128]{1,0:T(8,128)(2,1)}, u32[]{:S(2)}) copy-start(bf16[8192,128]{1,0:T(8,128)(2,1)} %param.15) | copy-start | bytes 6291460
  7.2 92.6 %all-gather.11.cloned.1.call-start = ((), (), s32[]{:S(2)}) async-start(), calls=%async_computation.2 | async-start | bytes 1064960 | tf_op jit(solution)/shard_map/all_gather | solution.py:50
  7.9 177.6 %all-gather.15.cloned.1.call-start = ((), (), s32[]{:S(2)}) async-start(), calls=%async_computation.4 | async-start | bytes 3194880 | tf_op jit(solution)/shard_map/all_gather | solution.py:74
  12.6 257.7 %all-gather.13.cloned.1.call-start = ((), (), s32[]{:S(2)}) async-start(), calls=%async_computation.3 | async-start | bytes 3194880 | tf_op jit(solution)/shard_map/all_gather | solution.py:75
  13.3 346.8 %all-gather.9.cloned.1.call-start = ((), (), s32[]{:S(2)}) async-start(), calls=%async_computation.1 | async-start | bytes 8519680 | tf_op jit(solution)/shard_map/all_gather | solution.py:49
  13.9 175.3 %copy-start.2 = (bf16[16,64,128]{2,1,0:T(8,128)(2,1)S(1)}, bf16[16,64,128]{2,1,0:T(8,128)(2,1)}, u32[]{:S(2)}) copy-start(bf16[16,64,128]{2,1,0:T(8,128)(2,1)} %param.18) | copy-start | bytes 786436
  13.9 175.3 %copy-start.8 = (bf16[16,4,128]{2,1,0:T(4,128)(2,1)S(1)}, bf16[16,4,128]{2,1,0:T(4,128)(2,1)}, u32[]{:S(2)}) copy-start(bf16[16,4,128]{2,1,0:T(4,128)(2,1)} %param.17) | copy-start | bytes 49156
  13.9 382.3 %all-gather.7.cloned.1.call-start = ((), (), s32[]{:S(2)}) async-start(), calls=%async_computation | async-start | bytes 1179648 | tf_op jit(solution)/shard_map/all_gather | solution.py:42
  86.1 103.1 %copy-start.6 = (pred[16]{0:T(512)(128)(4,1)}, pred[16]{0:T(512)(128)(4,1)S(1)}, u32[]{:S(2)}) copy-start(pred[16]{0:T(512)(128)(4,1)S(1)} %fusion.34) | copy-start | bytes 52
  87.1 102.1 %copy-start.4 = (pred[16,64]{1,0:T(8,128)(4,1)}, pred[16,64]{1,0:T(8,128)(4,1)S(1)}, u32[]{:S(2)}) copy-start(pred[16,64]{1,0:T(8,128)(4,1)S(1)} %fusion.28) | copy-start | bytes 3076
  189.8 182.8 %copy-start.1 = (bf16[16,64,128]{2,1,0:T(8,128)(2,1)}, bf16[16,64,128]{2,1,0:T(8,128)(2,1)S(1)}, u32[]{:S(2)}) copy-start(bf16[16,64,128]{2,1,0:T(8,128)(2,1)S(1)} %fusion.11) | copy-start | bytes 786436
  372.6 25.4 %copy-start.3 = (bf16[16,64,128]{2,1,0:T(8,128)(2,1)S(1)}, bf16[16,64,128]{2,1,0:T(8,128)(2,1)}, u32[]{:S(2)}) copy-start(bf16[16,64,128]{2,1,0:T(8,128)(2,1)} %param.19) | copy-start | bytes 786436
  372.6 25.4 %copy-start.5 = (pred[16,64]{1,0:T(8,128)(4,1)S(1)}, pred[16,64]{1,0:T(8,128)(4,1)}, u32[]{:S(2)}) copy-start(pred[16,64]{1,0:T(8,128)(4,1)} %copy-done.4) | copy-start | bytes 3076
  372.6 25.4 %copy-start.7 = (pred[16]{0:T(512)(128)(4,1)S(1)}, pred[16]{0:T(512)(128)(4,1)}, u32[]{:S(2)}) copy-start(pred[16]{0:T(512)(128)(4,1)} %copy-done.6) | copy-start | bytes 52
  398.6 1.0 copy-start.9
Sparse Core Ops, SparseCore 0:
  11.4 88.3 all-gather.10
  103.7 81.7 all-gather.14
  188.9 81.3 all-gather.12
  273.5 86.5 all-gather.8
  362.6 32.8 all-gather.6
where the time goes:
time: 411 us; the launch traced here: 406 us
  waiting for transfers between devices  263 us (64%)
  blocking collectives  88.8 us (22%)
  matrix products  25.5 us (6%)
  between operations  14.7 us (4%)
  local copies, waits for them, and re-layouts  10.9 us (3%)
    all_gather x1, waiting for transfers between devices, body(): lax.all_gather(adapter_shrink, 'replica', axis=0, tiled=True)  86.1 us
    all_gather x1, waiting for transfers between devices, body(): lax.all_gather(out_keys, 'replica', axis=0, tiled=True)  83.9 us
    all_gather x1, waiting for transfers between devices, body(): lax.all_gather(out_values, 'replica', axis=0, tiled=True)  79.9 us
    all_gather x1, blocking collectives, body(): lax.all_gather(leaving[:, 1:3], 'replica', axis=0, tiled=True)  51.1 us
    psum x1, blocking collectives, body(): shrink = lax.psum(partial_value, 'tensor').astype(jnp.bfloat16)  23.2 us
    unnamed x1, blocking collectives  14.5 us
    dot_general x1, matrix products, body(): jnp.einsum('bk,kdr->bdr', chosen, whole_down, preferred_element_type=jnp....  12.5 us
    all_gather x1, waiting for transfers between devices, body(): lax.all_gather(adapter_expand, 'replica', axis=0, tiled=True)  10.8 us
  transfers between devices with their start and end apart: 5, of which 4 were waited for; matrix products, arithmetic and copies ran while one was open for 9% of the time, Pallas kernels for 0%

commit v1 on v0

v1 whole, which is shorter than its diff:
```python
import functools
import math

import jax
import jax.numpy as jnp
from jax import lax
from jax.experimental import pallas as pl
from jax.experimental.pallas import tpu as pltpu
from jax.sharding import PartitionSpec as P

NZ, NX, NC, NY = 8, 4, 2, 8
PLANE = NX * NC
REPLICAS = NZ * PLANE
MESH = pl.DeviceIdType.MESH
F32, BF16 = jnp.float32, jnp.bfloat16

SLOTS, STEPS, BLOCKS, CACHE, HD, RANK = 16, 4, 4, 64, 128, 64
ROWS = SLOTS * STEPS
PART = 1024
HALF = ROWS // 2
MIG_ROWS = 2 * CACHE + 16
COPIES = 110

SHRINK_AT = {1: 0, 7: 1, 2: 2, 6: 3, 3: 4, 5: 5, 0: 6, 4: 7}
EXPAND_AT = {1: 0, 7: 1, 2: 2, 6: 3, 0: 4, 3: 5, 5: 6, 4: 7}
NEAR = 5


def pick(table, index):
    out = jnp.int32(table[0])
    for key, value in table.items():
        if key:
            out = jnp.where(index == key, jnp.int32(value), out)
    return out


def lanes(shape):
    return lax.broadcasted_iota(jnp.int32, shape, len(shape) - 1)


def comm_kernel(
    tok_ref, w_hbm, keys_ref, values_ref, length_ref, mig_ref, index_ref, owner_ref, shrink_ref, expand_ref,
    fresh_ref, arrived_ref,
    w_ref, w_sem, tok_f32, tok_y, tok_x, shrink_z, expand_x, mig_out, mig_in, mig_x, mig_z,
    acc, part_out, part_x, part_y, send_sem, recv_sem,
):
    r, t = lax.axis_index("replica"), lax.axis_index("tensor")
    z, w = r // PLANE, r % PLANE
    x, c = w // NC, w % NC

    def along_z(d):
        return ((r + d * PLANE) % REPLICAS, t)

    def along_y(d):
        return (r, (t + d) % NY)

    def in_plane(dx, dc):
        return (z * PLANE + ((x + dx) % NX) * NC + (c + dc) % NC, t)

    copies = []

    def send(src, dst, device):
        k = len(copies)
        copy = pltpu.make_async_remote_copy(
            src_ref=src, dst_ref=dst, send_sem=send_sem.at[k], recv_sem=recv_sem.at[k],
            device_id=device, device_id_type=MESH,
        )
        copies.append(copy)
        copy.start()
        return copy

    load_w = pltpu.make_async_copy(w_hbm, w_ref, w_sem)
    load_w.start()

    barrier = pltpu.get_barrier_semaphore()
    others = [along_y(d) for d in range(1, NY)]
    others += [in_plane(dx, dc) for dx in range(NX) for dc in range(NC) if dx or dc]
    others += [along_z(1), along_z(-1), along_z(NZ // 2)]
    others += [((r + 1) % REPLICAS, t), ((r + REPLICAS - 1) % REPLICAS, t)]
    for other in others:
        pl.semaphore_signal(barrier, inc=1, device_id=other, device_id_type=MESH)

    for s in range(SLOTS):
        tok_f32[s * STEPS : (s + 1) * STEPS, :] = tok_ref[s].astype(F32)
    own = tok_f32[...].astype(BF16)
    tok_y[0] = own
    tok_x[0, :, 0:PART] = own
    row = lax.broadcasted_iota(jnp.int32, (ROWS, HD), 0)
    stored = [owner_ref[index_ref[0, b]] for b in range(BLOCKS)]
    stored_rows = jnp.zeros((ROWS, HD), F32)
    for b in range(BLOCKS):
        stored_rows = jnp.where(row // (ROWS // BLOCKS) == b, stored[b].astype(F32), stored_rows)
    tok_x[0, :, PART:] = stored_rows.astype(BF16)
    shrink_z[SHRINK_AT[0]] = shrink_ref[...]
    expand_x[0, EXPAND_AT[0]] = expand_ref[0]

    offsets = [(mig_ref[0, e, 1] - r + REPLICAS) % REPLICAS for e in range(3)]
    half = REPLICAS // 2
    fits = [
        [o == 1 for o in offsets],
        [o == half for o in offsets],
        [(o != 1) & (o != half) for o in offsets],
    ]

    def chosen(which, column):
        first, second, third = (column(e) for e in range(3))
        return jnp.where(fits[which][0], first, jnp.where(fits[which][1], second, third))

    other_offset = chosen(2, lambda e: offsets[e])
    mig_row = lax.broadcasted_iota(jnp.int32, (16, HD), 0)
    for which in range(3):
        slot = chosen(which, lambda e: mig_ref[0, e, 0])
        landing = chosen(which, lambda e: mig_ref[0, e, 2]).astype(F32)
        filled = length_ref[slot].astype(F32)
        notes = jnp.where(mig_row == 0, landing, filled).astype(BF16)
        mig_out[which, 0:CACHE] = keys_ref[slot]
        mig_out[which, CACHE : 2 * CACHE] = values_ref[slot]
        mig_out[which, 2 * CACHE :] = notes

    pl.semaphore_wait(barrier, len(others))

    def ring(n, right, left, parts, split):
        gone = {}
        for k in range(1, n // 2 + 1):
            stay = []
            for h, (at, last) in enumerate(zip(parts, split)):
                for way, device in ((-1, right), (1, left)):
                    if k == n // 2 and last != way:
                        stay.append(gone[k - 1, h, way])
                        continue
                    if k > 1:
                        gone[k - 1, h, way].wait_recv()
                    src, dst = way * (k - 1) % n, way * k % n
                    gone[k, h, way] = send(at(src), at(dst), device)
            for copy in stay:
                copy.wait_recv()
            yield k - 1
        for (k, _, _), copy in gone.items():
            if k == n // 2:
                copy.wait_recv()
        yield n // 2

    def finish(steps):
        for _ in steps:
            pass

    first_rows, last_rows = pl.ds(0, HALF), pl.ds(HALF, HALF)

    def shrink_part(rows):
        return lambda d: shrink_z.at[SHRINK_AT[d], rows]

    z_steps = ring(
        NZ, along_z(1), along_z(-1),
        [shrink_part(first_rows), shrink_part(last_rows), lambda d: expand_x.at[0, EXPAND_AT[d]]],
        [-1, 1, -1],
    )
    y_steps = ring(
        NY, along_y(1), along_y(-1),
        [lambda d: tok_y.at[d, first_rows], lambda d: tok_y.at[d, last_rows]],
        [-1, 1],
    )
    x_steps = ring(
        NX, in_plane(1, 0), in_plane(-1, 0),
        [lambda d: tok_x.at[d * NC, first_rows], lambda d: tok_x.at[d * NC, last_rows]],
        [-1, 1],
    )

    base = None

    def add_base(d):
        nonlocal base
        rows = pl.multiple_of((t + d) % NY * PART, PART)
        term = jnp.dot(tok_y[d], w_ref[pl.ds(rows, PART), :], preferred_element_type=F32)
        base = term if base is None else base + term

    next(z_steps)
    next(y_steps)
    next(x_steps)
    to_sibling = [send(tok_x.at[0], tok_x.at[1], in_plane(0, 1))]
    mig_sent = {}
    for dx in range(NX):
        for dc in range(NC):
            if dx or dc:
                back = (-dx % NX) * NC + dc
                mig_sent[dx, dc] = send(mig_out.at[2], mig_x.at[back], in_plane(dx, dc))
    straight = [
        send(mig_out.at[0], mig_in.at[0], ((r + 1) % REPLICAS, t)),
        send(mig_out.at[1], mig_in.at[1], along_z(half // PLANE)),
    ]
    mig_x[0] = mig_out[2]
    load_w.wait()
    add_base(0)

    next(z_steps)
    next(y_steps)
    next(x_steps)
    add_base(1)
    add_base(NY - 1)
    finish(x_steps)
    to_sibling += [send(tok_x.at[d * NC], tok_x.at[d * NC + 1], in_plane(0, 1)) for d in range(1, NX)]

    for copy in mig_sent.values():
        copy.wait_recv()
    plane_offset, z_offset = other_offset % PLANE, other_offset // PLANE
    from_w = (w - plane_offset + PLANE) % PLANE
    carry = jnp.where(from_w + plane_offset >= PLANE, 1, 0)
    from_slot = (from_w // NC - x + NX) % NX * NC + (from_w % NC - c + NC) % NC
    mig_z[0] = mig_x[from_slot]
    mig_steps = ring(
        NZ, along_z(1), along_z(-1),
        [lambda d: mig_z.at[d, pl.ds(0, CACHE)], lambda d: mig_z.at[d, pl.ds(CACHE, MIG_ROWS - CACHE)]],
        [-1, 1],
    )

    next(z_steps)
    next(y_steps)
    next(mig_steps)
    expand_sent = [
        [
            send(expand_x.at[0, pl.ds(0, NEAR)], expand_x.at[(-dx % NX) * NC, pl.ds(0, NEAR)], in_plane(dx, 0))
            for dx in range(1, NX)
        ]
    ]
    expand_sibling = [send(expand_x.at[0, pl.ds(0, NEAR)], expand_x.at[1, pl.ds(0, NEAR)], in_plane(0, 1))]
    add_base(2)
    add_base(NY - 2)

    next(z_steps)
    next(y_steps)
    next(mig_steps)
    for copy in to_sibling:
        copy.wait_recv()

    lane = lanes((1, HD))
    stored_all = tok_x[:, :, PART:].reshape(PLANE * ROWS, HD).astype(F32)

    def add_products(pair):
        both = shrink_z[2 * pair : 2 * pair + 2].reshape(2 * RANK, PART)
        product = lax.dot_general(
            tok_x[:, :, 0:PART].reshape(PLANE * ROWS, PART), both, (((1,), (1,)), ((), ())),
            preferred_element_type=F32,
        )
        first, second = (
            ((r + d * PLANE) % REPLICAS).astype(F32) for d, at in SHRINK_AT.items() if at // 2 == pair
        )
        mine = stored_all == jnp.where(lane < RANK, first, second)
        return jnp.where(mine, product, 0.0)

    acc[...] = add_products(0)
    acc[...] += add_products(1)
    add_base(3)
    add_base(NY - 3)
    for dx in range(1, NX):
        expand_sent[0][dx - 1].wait_recv()
        at = -dx % NX * NC
        src = expand_x.at[at, pl.ds(0, NEAR)]
        expand_sibling.append(send(src, expand_x.at[at + 1, pl.ds(0, NEAR)], in_plane(0, 1)))
    next(mig_steps)
    acc[...] += add_products(2)
    next(z_steps)

    far = pl.ds(NEAR, NZ - NEAR)
    far_sent = [
        send(expand_x.at[0, far], expand_x.at[(-dx % NX) * NC, far], in_plane(dx, 0)) for dx in range(1, NX)
    ]
    expand_sibling.append(send(expand_x.at[0, far], expand_x.at[1, far], in_plane(0, 1)))

    total = (acc[...] + add_products(3)).reshape(PLANE, ROWS, HD)
    total = total + jnp.concatenate([total[:, :, RANK:], total[:, :, :RANK]], axis=-1)
    part_out[...] = jnp.where(lanes((PLANE, HALF, HD)) < RANK, total[:, :HALF], total[:, HALF:])
    part_sent = []
    for dx in range(NX):
        for dc in range(NC):
            if dx or dc:
                back = (-dx % NX) * NC + dc
                part_sent.append(send(part_out.at[dx * NC + dc], part_x.at[back], in_plane(dx, dc)))
    part_x[0] = part_out[0]
    next(y_steps)
    add_base(4)
    next(mig_steps)
    for copy in part_sent:
        copy.wait_recv()
    part_y[0] = jnp.sum(part_x[...], axis=0)
    over_y = [send(part_y.at[0], part_y.at[NY - d], along_y(d)) for d in range(1, NY)]
    for dx in range(1, NX):
        far_sent[dx - 1].wait_recv()
        at = -dx % NX * NC
        expand_sibling.append(send(expand_x.at[at, far], expand_x.at[at + 1, far], in_plane(0, 1)))
    next(mig_steps)
    from_z = pick({d: d for d in range(NZ)}, (2 * NZ - z_offset - carry) % NZ)
    arrived_ref[2] = mig_z[from_z]
    for k, copy in enumerate(straight):
        copy.wait_recv()
        arrived_ref[k] = mig_in[k]
    for copy in expand_sibling:
        copy.wait_recv()
    expands = []
    for b in range(BLOCKS):
        oz, ow = stored[b] // PLANE, stored[b] % PLANE
        at = (ow // NC - x + NX) % NX * NC + (ow % NC - c + NC) % NC
        expands.append(expand_x[at, pick(EXPAND_AT, (oz - z + NZ) % NZ)])
    for copy in over_y:
        copy.wait_recv()
    shrink = jnp.sum(part_y[...], axis=0).astype(BF16)
    rows = ROWS // BLOCKS
    lane16 = lanes((rows, HD))
    deltas = [None] * BLOCKS
    for k in range(2):
        mine = shrink[k * rows : (k + 1) * rows].astype(F32)
        left = jnp.where(lane16 < RANK, mine, 0.0)
        right = jnp.where(lane16 < RANK, 0.0, mine)
        both = jnp.concatenate([expands[k], expands[k + 2]], axis=0)
        out = jnp.dot(jnp.concatenate([left, right], axis=0).astype(BF16), both, preferred_element_type=F32)
        deltas[k], deltas[k + 2] = out[:rows], out[rows:]
    fresh_ref[...] = (base + jnp.concatenate(deltas, axis=0)).astype(BF16)

    for copy in copies:
        copy.wait_send()


def attend_kernel(q_ref, draft_ref, keys_ref, values_ref, length_ref, arrived_ref, fresh_ref, out_ref, ko_ref, vo_ref):
    group = q_ref.shape[2] // HD
    heads = group * STEPS
    spot = lax.broadcasted_iota(jnp.int32, (CACHE, HD), 0).astype(F32)
    landing = [arrived_ref[a, 2 * CACHE : 2 * CACHE + 1, :].astype(F32) for a in range(3)]
    lengths = [arrived_ref[a, 2 * CACHE + 1 : 2 * CACHE + 2, :].astype(F32) for a in range(3)]
    fresh = fresh_ref[...].astype(F32)
    lane = lanes((1, HD))
    row_at = lax.broadcasted_iota(jnp.int32, (2 * heads, HD), 0)
    lane_at = lanes((2 * heads, HD))
    same = (row_at // heads) == (lane_at // CACHE)
    ahead = (lane_at % CACHE - row_at % STEPS).astype(F32)
    scale = 1.0 / math.sqrt(HD)

    for pair in range(SLOTS // 2):
        filled, queries = [], []
        for s in (2 * pair, 2 * pair + 1):
            here = [landing[a] == float(s) for a in range(3)]
            fill = jnp.full((1, HD), length_ref[s].astype(F32))
            key, value = keys_ref[s].astype(F32), values_ref[s].astype(F32)
            for a in range(3):
                fill = jnp.where(here[a], lengths[a], fill)
                key = jnp.where(here[a], arrived_ref[a, :CACHE].astype(F32), key)
                value = jnp.where(here[a], arrived_ref[a, CACHE : 2 * CACHE].astype(F32), value)
            after = spot - fill
            draft = draft_ref[s].astype(F32)
            for j in range(STEPS):
                key = jnp.where(after == float(j), draft[j : j + 1], key)
                value = jnp.where(after == float(j), fresh[s * STEPS + j : s * STEPS + j + 1], value)
            ko_ref[s] = key.astype(BF16)
            vo_ref[s] = value.astype(BF16)
            filled.append(fill)
            query = q_ref[s].astype(F32)
            queries += [query[:, g * HD : (g + 1) * HD] for g in range(group)]
        stacked = jnp.concatenate(queries, axis=0).astype(BF16)
        both_keys = ko_ref[2 * pair : 2 * pair + 2].reshape(2 * CACHE, HD)
        both_values = vo_ref[2 * pair : 2 * pair + 2].reshape(2 * CACHE, HD)
        scores = lax.dot_general(stacked, both_keys, (((1,), (1,)), ((), ())), preferred_element_type=F32) * scale
        allowed = same & (ahead <= jnp.where(lane < CACHE, filled[0], filled[1]))
        masked = jnp.where(allowed, scores, -1e30)
        top = jnp.max(masked, axis=-1, keepdims=True)
        raised = jnp.where(allowed, jnp.exp(masked - top), 0.0)
        weights = (raised / jnp.sum(raised, axis=-1, keepdims=True)).astype(BF16)
        attended = jnp.dot(weights, both_values, preferred_element_type=F32)
        for k in range(2):
            for g in range(group):
                at = k * heads + g * STEPS
                out_ref[2 * pair + k, :, g * HD : (g + 1) * HD] = attended[at : at + STEPS].astype(BF16)


def body(
    tokens,
    value_matrix,
    queries,
    draft_keys,
    key_cache_before,
    value_cache_before,
    cache_length,
    migrations,
    block_adapter_index,
    adapter_replica,
    adapter_shrink,
    adapter_expand,
):
    vmem = pl.BlockSpec(memory_space=pltpu.VMEM)
    smem = pl.BlockSpec(memory_space=pltpu.SMEM)
    fresh, arrived = pl.pallas_call(
        comm_kernel,
        out_shape=(
            jax.ShapeDtypeStruct((ROWS, HD), BF16),
            jax.ShapeDtypeStruct((3, MIG_ROWS, HD), BF16),
        ),
        in_specs=[vmem, pl.BlockSpec(memory_space=pl.ANY), vmem, vmem, smem, smem, smem, smem, vmem, vmem],
        out_specs=(vmem, vmem),
        scratch_shapes=[
            pltpu.VMEM(value_matrix.shape, BF16),
            pltpu.SemaphoreType.DMA,
            pltpu.VMEM((ROWS, PART), F32),
            pltpu.VMEM((NY, ROWS, PART), BF16),
            pltpu.VMEM((PLANE, ROWS, PART + HD), BF16),
            pltpu.VMEM((NZ, RANK, PART), BF16),
            pltpu.VMEM((PLANE, NZ, RANK, HD), BF16),
            pltpu.VMEM((3, MIG_ROWS, HD), BF16),
            pltpu.VMEM((2, MIG_ROWS, HD), BF16),
            pltpu.VMEM((PLANE, MIG_ROWS, HD), BF16),
            pltpu.VMEM((NZ, MIG_ROWS, HD), BF16),
            pltpu.VMEM((PLANE * ROWS, HD), F32),
            pltpu.VMEM((PLANE, HALF, HD), F32),
            pltpu.VMEM((PLANE, HALF, HD), F32),
            pltpu.VMEM((NY, HALF, HD), F32),
            pltpu.SemaphoreType.DMA((COPIES,)),
            pltpu.SemaphoreType.DMA((COPIES,)),
        ],
        compiler_params=pltpu.CompilerParams(
            collective_id=0, has_side_effects=True, vmem_limit_bytes=48 * 1024 * 1024
        ),
        name="gather_and_project",
    )(
        tokens,
        value_matrix,
        key_cache_before,
        value_cache_before,
        cache_length,
        migrations,
        block_adapter_index,
        adapter_replica,
        jnp.swapaxes(adapter_shrink[0], 0, 1),
        adapter_expand,
    )
    return pl.pallas_call(
        attend_kernel,
        out_shape=(
            jax.ShapeDtypeStruct(queries.shape, BF16),
            jax.ShapeDtypeStruct(key_cache_before.shape, BF16),
            jax.ShapeDtypeStruct(value_cache_before.shape, BF16),
        ),
        in_specs=[vmem, vmem, vmem, vmem, smem, vmem, vmem],
        out_specs=(vmem, vmem, vmem),
        compiler_params=pltpu.CompilerParams(vmem_limit_bytes=48 * 1024 * 1024),
        name="place_and_attend",
    )(queries, draft_keys, key_cache_before, value_cache_before, cache_length, arrived, fresh)


def solution(mesh):
    placed = (
        P("replica", None, "tensor"),
        P(None, "tensor"),
        P("replica", None, "tensor"),
        P("replica", None, "tensor"),
        P("replica", None, "tensor"),
        P("replica", None, "tensor"),
        P("replica"),
        P("replica", None, None),
        P("replica", None),
        P(),
        P("replica", "tensor", None),
        P("replica", None, "tensor"),
    )
    return jax.shard_map(
        body,
        mesh=mesh,
        in_specs=placed,
        out_specs=(
            P("replica", None, "tensor"),
            P("replica", None, "tensor"),
            P("replica", None, "tensor"),
        ),
        check_vma=False,
    )
```

time: 411 us -> 63.4 us (0.15); the launches traced: 406 us -> 63.1 us
  waiting for transfers between devices: 263 us -> 0 us
  blocking collectives: 88.8 us -> 0 us
  Pallas kernels: 0 us -> 53.8 us
  matrix products: 25.5 us -> 0 us
  between operations: 14.7 us -> 0.66 us
    all_gather x5 -> x0, waiting for transfers between devices: 261 us -> none  [the longest x1 86.1 us: body(): lax.all_gather(adapter_shrink, 'replica', axis=0, tiled=True)]
    pallas_call x0 -> x2, Pallas kernels: none -> 53.8 us  [the longest x1 49.9 us: body(): pl.pallas_call(comm_kernel, out_shape=(jax.ShapeDtypeStruct((ROWS, HD), B...]
    all_gather x1 -> x0, blocking collectives: 51.1 us -> none  [body(): lax.all_gather(leaving[:, 1:3], 'replica', axis=0, tiled=True)]
    dot_general x11 -> x0, matrix products: 25.5 us -> none  [the longest x1 12.5 us: body(): jnp.einsum('bk,kdr->bdr', chosen, whole_down, preferred_element_type=jnp....]
    psum x1 -> x0, blocking collectives: 23.2 us -> none  [body(): shrink = lax.psum(partial_value, 'tensor').astype(jnp.bfloat16)]
    unnamed x1 -> x0, blocking collectives: 14.5 us -> none
    unnamed x24 -> x23, local copies, waits for them, and re-layouts: 2.15 us -> 8.67 us
    gather x3 -> x0, local copies, waits for them, and re-layouts: 4.32 us -> none  [the longest x1 1.51 us: body(): out_keys = jnp.take(key_cache_before, leaving[:, 0], axis=0)]
  transfers between devices with their start and end apart: 5 -> 0, of which waited for: 4 -> 0; matrix products, arithmetic and copies ran while one was open for 9% -> 0% of each run, Pallas kernels for 0% -> 0%
where the time goes in v1:
time: 63.4 us; the launch traced here: 63.1 us
  Pallas kernels  53.8 us (85%)
  local copies, waits for them, and re-layouts  8.67 us (14%)
  between operations  0.66 us (1%)
    pallas_call x1, Pallas kernels, body(): pl.pallas_call(comm_kernel, out_shape=(jax.ShapeDtypeStruct((ROWS, HD), B...  49.9 us
    unnamed x23, local copies, waits for them, and re-layouts  8.67 us
    pallas_call x1, Pallas kernels, body(): pl.pallas_call(attend_kernel, out_shape=(jax.ShapeDtypeStruct(queries.sha...  3.91 us

profile of v1, /device:TPU:1, one launch (start us, length us, event | category | flops | bytes accessed | tf_op | source)
XLA Modules:
  0.0 63.1 jit_solution(11780022716623964140)
XLA Ops:
  0.6 0.7 %copy.15.mig_ref = s32[1,3,3]{2,1,0:T(4,128)S(1)} copy(s32[1,3,3]{2,0,1:T(1,128)} %param.19) | data formatting | bytes 72 | tf_op args[7]
  1.3 0.0 copy-start
  1.3 1.6 %copy-done = bf16[8192,128]{1,0:T(8,128)(2,1)S(1)} copy-done((bf16[8192,128]{1,0:T(8,128)(2,1)S(1)}, bf16[8192,128]{1,0:T(8,128)(2,1)}, u32[]{:S(2)}) %copy-start) | copy-done | bytes 2097176
  2.9 0.0 copy-start.1
  2.9 0.9 %copy-done.1 = bf16[16,64,128]{2,1,0:T(8,128)(2,1)S(1)} copy-done((bf16[16,64,128]{2,1,0:T(8,128)(2,1)S(1)}, bf16[16,64,128]{2,1,0:T(8,128)(2,1)}, u32[]{:S(2)}) %copy-start.1) | copy-done | bytes 262168
  3.9 0.0 copy-start.2
  3.9 0.9 %copy-done.2 = bf16[16,64,128]{2,1,0:T(8,128)(2,1)S(1)} copy-done((bf16[16,64,128]{2,1,0:T(8,128)(2,1)S(1)}, bf16[16,64,128]{2,1,0:T(8,128)(2,1)}, u32[]{:S(2)}) %copy-start.2) | copy-done | bytes 262168
  4.8 0.0 copy-start.3
  4.8 0.9 %copy-done.3 = bf16[16,4,1024]{2,1,0:T(4,128)(2,1)S(1)} copy-done((bf16[16,4,1024]{2,1,0:T(4,128)(2,1)S(1)}, bf16[16,4,1024]{2,1,0:T(4,128)(2,1)}, u32[]{:S(2)}) %copy-start.3) | copy-done | bytes 131096
  5.7 0.0 copy-start.4
  5.7 0.9 %copy-done.4 = bf16[1,1024,64]{1,2,0:T(8,128)(2,1)S(1)} copy-done((bf16[1,1024,64]{1,2,0:T(8,128)(2,1)S(1)}, bf16[1,1024,64]{1,2,0:T(8,128)(2,1)}, u32[]{:S(2)}) %copy-start.4) | copy-done | bytes 131096
  6.6 0.0 copy-start.6
  6.6 0.7 %copy-done.6 = bf16[1,64,128]{2,1,0:T(8,128)(2,1)S(1)} copy-done((bf16[1,64,128]{2,1,0:T(8,128)(2,1)S(1)}, bf16[1,64,128]{2,1,0:T(8,128)(2,1)}, u32[]{:S(2)}) %copy-start.6) | copy-done | bytes 16408
  7.3 0.0 copy-start.8
  7.3 0.7 %copy-done.8 = s32[16]{0:T(128)S(1)} copy-done((s32[16]{0:T(128)S(1)}, s32[16]{0:T(128)}, u32[]{:S(2)}) %copy-start.8) | copy-done | bytes 88
  8.0 0.0 copy-start.9
  8.0 0.7 %copy-done.9 = s32[1,4]{1,0:T(1,128)S(1)} copy-done((s32[1,4]{1,0:T(1,128)S(1)}, s32[1,4]{1,0:T(1,128)}, u32[]{:S(2)}) %copy-start.9) | copy-done | bytes 40
  8.6 0.0 copy-start.10
  8.6 0.7 %copy-done.10 = s32[64]{0:T(128)S(1)} copy-done((s32[64]{0:T(128)S(1)}, s32[64]{0:T(128)}, u32[]{:S(2)}) %copy-start.10) | copy-done | bytes 280
  9.3 0.0 copy-start.5
  9.3 0.0 copy-start.7
  9.3 49.9 %gather_and_project.1 = (bf16[64,128]{1,0:T(8,128)(2,1)S(1)}, bf16[3,144,128]{2,1,0:T(8,128)(2,1)S(1)}) custom-call(bf16[16,4,1024]{2,1,0:T(4,128)(2,1)S(1)} %copy-done.3, bf16[8192,128]{1,0:T(8,128)(2,1)S(1)} %copy-done, bf16[16,64,128]{2,1,0:T(8,128)(2,1)S(1)} %copy-done.1, bf16[16,64,128]{2,1,0:T(8,128)(2,1)S(1)} %copy-done.2, s32[16]{0:T(128)S(1)} %copy-done.8, ...), custom_call_target="tpu_custom_call" | custom-call | tf_op jit(solution)/shard_map/gather_and_project/pallas_call | solution.py:387
  59.2 0.0 copy-done.5
  59.2 0.0 copy-done.7
  59.2 3.9 %place_and_attend.1 = (bf16[16,4,1024]{2,1,0:T(4,128)(2,1)}, bf16[16,64,128]{2,1,0:T(8,128)(2,1)}, bf16[16,64,128]{2,1,0:T(8,128)(2,1)}) custom-call(bf16[16,4,1024]{2,1,0:T(4,128)(2,1)S(1)} %copy-done.5, bf16[16,4,128]{2,1,0:T(4,128)(2,1)S(1)} %copy-done.7, bf16[16,64,128]{2,1,0:T(8,128)(2,1)S(1)} %copy-done.1, bf16[16,64,128]{2,1,0:T(8,128)(2,1)S(1)} %copy-done.2, ...), custom_call_target="tpu_custom_call" | custom-call | tf_op jit(solution)/shard_map/place_and_attend/pallas_call | solution.py:430
Async XLA Ops:
  1.3 1.6 %copy-start = (bf16[8192,128]{1,0:T(8,128)(2,1)S(1)}, bf16[8192,128]{1,0:T(8,128)(2,1)}, u32[]{:S(2)}) copy-start(bf16[8192,128]{1,0:T(8,128)(2,1)} %w_hbm.1) | copy-start | bytes 6291460
  2.9 0.9 %copy-start.1 = (bf16[16,64,128]{2,1,0:T(8,128)(2,1)S(1)}, bf16[16,64,128]{2,1,0:T(8,128)(2,1)}, u32[]{:S(2)}) copy-start(bf16[16,64,128]{2,1,0:T(8,128)(2,1)} %keys_ref.3) | copy-start | bytes 786436
  3.9 0.9 %copy-start.2 = (bf16[16,64,128]{2,1,0:T(8,128)(2,1)S(1)}, bf16[16,64,128]{2,1,0:T(8,128)(2,1)}, u32[]{:S(2)}) copy-start(bf16[16,64,128]{2,1,0:T(8,128)(2,1)} %values_ref.3) | copy-start | bytes 786436
  4.8 0.9 %copy-start.3 = (bf16[16,4,1024]{2,1,0:T(4,128)(2,1)S(1)}, bf16[16,4,1024]{2,1,0:T(4,128)(2,1)}, u32[]{:S(2)}) copy-start(bf16[16,4,1024]{2,1,0:T(4,128)(2,1)} %tok_ref.1) | copy-start | bytes 393220
  5.7 0.9 %copy-start.4 = (bf16[1,1024,64]{1,2,0:T(8,128)(2,1)S(1)}, bf16[1,1024,64]{1,2,0:T(8,128)(2,1)}, u32[]{:S(2)}) copy-start(bf16[1,1024,64]{1,2,0:T(8,128)(2,1)} %param.22) | copy-start | bytes 393220
  6.6 0.7 %copy-start.6 = (bf16[1,64,128]{2,1,0:T(8,128)(2,1)S(1)}, bf16[1,64,128]{2,1,0:T(8,128)(2,1)}, u32[]{:S(2)}) copy-start(bf16[1,64,128]{2,1,0:T(8,128)(2,1)} %expand_ref.1) | copy-start | bytes 49156
  7.3 0.7 %copy-start.8 = (s32[16]{0:T(128)S(1)}, s32[16]{0:T(128)}, u32[]{:S(2)}) copy-start(s32[16]{0:T(128)} %length_ref.3) | copy-start | bytes 196
  8.0 0.7 %copy-start.9 = (s32[1,4]{1,0:T(1,128)S(1)}, s32[1,4]{1,0:T(1,128)}, u32[]{:S(2)}) copy-start(s32[1,4]{1,0:T(1,128)} %index_ref.1) | copy-start | bytes 52
  8.6 0.7 %copy-start.10 = (s32[64]{0:T(128)S(1)}, s32[64]{0:T(128)}, u32[]{:S(2)}) copy-start(s32[64]{0:T(128)} %owner_ref.1) | copy-start | bytes 772
  9.3 49.9 %copy-start.5 = (bf16[16,4,1024]{2,1,0:T(4,128)(2,1)S(1)}, bf16[16,4,1024]{2,1,0:T(4,128)(2,1)}, u32[]{:S(2)}) copy-start(bf16[16,4,1024]{2,1,0:T(4,128)(2,1)} %q_ref.1) | copy-start | bytes 393220
  9.3 49.9 %copy-start.7 = (bf16[16,4,128]{2,1,0:T(4,128)(2,1)S(1)}, bf16[16,4,128]{2,1,0:T(4,128)(2,1)}, u32[]{:S(2)}) copy-start(bf16[16,4,128]{2,1,0:T(4,128)(2,1)} %draft_ref.1) | copy-start | bytes 49156

commit v2 on v1

v2 whole, which is shorter than its diff:
```python
import math

import jax
import jax.numpy as jnp
from jax import lax
from jax.experimental import pallas as pl
from jax.experimental.pallas import tpu as pltpu
from jax.sharding import PartitionSpec as P

NZ, NX, NC, NY = 8, 4, 2, 8
PLANE = NX * NC
REPLICAS = NZ * PLANE
MESH = pl.DeviceIdType.MESH
F32, BF16 = jnp.float32, jnp.bfloat16

SLOTS, STEPS, BLOCKS, CACHE, HD, RANK = 16, 4, 4, 64, 128, 64
ROWS = SLOTS * STEPS
PART = 1024
HALF = ROWS // 2
MIG_ROWS = 2 * CACHE + 16
COPIES = 128

SHRINK_AT = {1: 0, 7: 1, 2: 2, 6: 3, 3: 4, 5: 5, 0: 6, 4: 7}
EXPAND_AT = {1: 0, 7: 1, 2: 2, 6: 3, 0: 4, 3: 5, 5: 6, 4: 7}
NEAR = 5


def pick(table, index):
    out = jnp.int32(table[0])
    for key, value in table.items():
        if key:
            out = jnp.where(index == key, jnp.int32(value), out)
    return out


def lanes(shape):
    return lax.broadcasted_iota(jnp.int32, shape, len(shape) - 1)


def comm_kernel(
    tok_hbm, w_hbm, keys_hbm, values_hbm, length_hbm, mig_hbm, index_hbm, owner_hbm, shrink_hbm, expand_hbm,
    fresh_ref, arrived_ref,
    tok_ref, w_ref, keys_ref, values_ref, length_ref, mig_ref, index_ref, owner_ref, load_sem, tok_f32,
    tok_y, tok_x, shrink_z, expand_x, mig_out, mig_in, mig_x, mig_z,
    acc, part_out, part_x, part_y, send_sem, recv_sem,
):
    r, t = lax.axis_index("replica"), lax.axis_index("tensor")
    z, w = r // PLANE, r % PLANE
    x, c = w // NC, w % NC

    def along_z(d):
        return ((r + d * PLANE) % REPLICAS, t)

    def along_y(d):
        return (r, (t + d) % NY)

    def in_plane(dx, dc):
        return (z * PLANE + ((x + dx) % NX) * NC + (c + dc) % NC, t)

    sibling = in_plane(0, 1)
    copies = []

    def send(src, dst, device):
        k = len(copies)
        copy = pltpu.make_async_remote_copy(
            src_ref=src, dst_ref=dst, send_sem=send_sem.at[k], recv_sem=recv_sem.at[k],
            device_id=device, device_id_type=MESH,
        )
        copies.append(copy)
        copy.start()
        return copy

    barrier = pltpu.get_barrier_semaphore()
    others = [along_z(1), along_z(-1), along_z(NZ // 2)]
    others += [along_y(d) for d in range(1, NY)]
    others += [in_plane(dx, dc) for dx in range(NX) for dc in range(NC) if dx or dc]
    others += [((r + 1) % REPLICAS, t), ((r + REPLICAS - 1) % REPLICAS, t)]
    for other in others:
        pl.semaphore_signal(barrier, inc=1, device_id=other, device_id_type=MESH)

    loads = [
        pltpu.make_async_copy(src, dst, load_sem.at[k])
        for k, (src, dst) in enumerate([
            (tok_hbm, tok_ref),
            (index_hbm, index_ref),
            (owner_hbm, owner_ref),
            (mig_hbm, mig_ref),
            (length_hbm, length_ref),
            (keys_hbm, keys_ref),
            (values_hbm, values_ref),
            (shrink_hbm, shrink_z.at[SHRINK_AT[0]]),
            (expand_hbm.at[0], expand_x.at[0, EXPAND_AT[0]]),
            (w_hbm, w_ref),
        ])
    ]
    for load in loads:
        load.start()
    tok_loads, mig_loads, late_loads = loads[:3], loads[3:7], loads[7:]

    def ring(n, right, left, parts, split):
        gone = {}
        for k in range(1, n // 2 + 1):
            stay = []
            for h, (at, last) in enumerate(zip(parts, split)):
                for way, device in ((-1, right), (1, left)):
                    if k == n // 2 and last != way:
                        stay.append(gone[k - 1, h, way])
                        continue
                    if k > 1:
                        gone[k - 1, h, way].wait_recv()
                    src, dst = way * (k - 1) % n, way * k % n
                    gone[k, h, way] = send(at(src, k == 1), at(dst, False), device)
            for copy in stay:
                copy.wait_recv()
            yield k - 1
        for (k, _, _), copy in gone.items():
            if k == n // 2:
                copy.wait_recv()
        yield n // 2

    def finish(steps):
        for _ in steps:
            pass

    first_rows, last_rows = pl.ds(0, HALF), pl.ds(HALF, HALF)

    def shrink_part(rows):
        return lambda d, own: shrink_hbm.at[rows] if own else shrink_z.at[SHRINK_AT[d], rows]

    z_steps = ring(
        NZ, along_z(1), along_z(-1),
        [
            lambda d, own: expand_hbm.at[0] if own else expand_x.at[0, EXPAND_AT[d]],
            shrink_part(first_rows),
            shrink_part(last_rows),
        ],
        [-1, -1, 1],
    )
    y_steps = ring(
        NY, along_y(1), along_y(-1),
        [lambda d, own: tok_y.at[d, first_rows], lambda d, own: tok_y.at[d, last_rows]],
        [-1, 1],
    )

    def x_ring(parts):
        return ring(NX, in_plane(1, 0), in_plane(-1, 0), parts, [-1, 1])

    x_steps = x_ring(
        [lambda d, own: tok_x.at[d * NC, first_rows], lambda d, own: tok_x.at[d * NC, last_rows]]
    )
    mig_halves = pl.ds(0, CACHE), pl.ds(CACHE, MIG_ROWS - CACHE)
    mig_x_steps = x_ring(
        [lambda d, own: mig_x.at[d * NC, mig_halves[0]], lambda d, own: mig_x.at[d * NC, mig_halves[1]]]
    )
    mig_steps = ring(
        NZ, along_z(1), along_z(-1),
        [lambda d, own: mig_z.at[d, mig_halves[0]], lambda d, own: mig_z.at[d, mig_halves[1]]],
        [-1, 1],
    )

    def expand_ring(first, middle, last):
        early, late = pl.ds(first, middle - first), pl.ds(middle, last - middle)
        return x_ring([lambda d, own: expand_x.at[d * NC, early], lambda d, own: expand_x.at[d * NC, late]])

    near_steps = expand_ring(0, 3, NEAR)
    far_steps = expand_ring(NEAR, NZ - 1, NZ)

    def to_sibling(at):
        return lambda d: send(at(d * NC), at(d * NC + 1), sibling)

    tokens_over = to_sibling(lambda at: tok_x.at[at])
    mig_over = to_sibling(lambda at: mig_x.at[at])
    near_over = to_sibling(lambda at: expand_x.at[at, pl.ds(0, NEAR)])
    far_over = to_sibling(lambda at: expand_x.at[at, pl.ds(NEAR, NZ - NEAR)])

    base = None

    def add_base(d):
        nonlocal base
        rows = pl.multiple_of((t + d) % NY * PART, PART)
        term = jnp.dot(tok_y[d], w_ref[pl.ds(rows, PART), :], preferred_element_type=F32)
        base = term if base is None else base + term

    pl.semaphore_wait(barrier, len(others))
    next(z_steps)

    for load in tok_loads:
        load.wait()
    for s in range(SLOTS):
        tok_f32[s * STEPS : (s + 1) * STEPS, :] = tok_ref[s].astype(F32)
    own = tok_f32[...].astype(BF16)
    tok_y[0] = own
    next(y_steps)
    tok_x[0, :, 0:PART] = own
    row = lax.broadcasted_iota(jnp.int32, (ROWS, HD), 0)
    stored = [owner_ref[index_ref[0, b]] for b in range(BLOCKS)]
    stored_rows = jnp.zeros((ROWS, HD), F32)
    for b in range(BLOCKS):
        stored_rows = jnp.where(row // (ROWS // BLOCKS) == b, stored[b].astype(F32), stored_rows)
    tok_x[0, :, PART:] = stored_rows.astype(BF16)
    next(x_steps)
    tokens_sent = [tokens_over(0)]

    for load in mig_loads:
        load.wait()
    offsets = [(mig_ref[e, 0, 1] - r + REPLICAS) % REPLICAS for e in range(3)]
    half = REPLICAS // 2
    fits = [
        [o == 1 for o in offsets],
        [o == half for o in offsets],
        [(o != 1) & (o != half) for o in offsets],
    ]

    def chosen(which, column):
        first, second, third = (column(e) for e in range(3))
        return jnp.where(fits[which][0], first, jnp.where(fits[which][1], second, third))

    other_offset = chosen(2, lambda e: offsets[e])
    mig_row = lax.broadcasted_iota(jnp.int32, (16, HD), 0)
    for which in range(3):
        slot = chosen(which, lambda e: mig_ref[e, 0, 0])
        landing = chosen(which, lambda e: mig_ref[e, 0, 2]).astype(F32)
        filled = length_ref[slot].astype(F32)
        notes = jnp.where(mig_row == 0, landing, filled).astype(BF16)
        out = mig_x.at[0] if which == 2 else mig_out.at[which]
        out[0:CACHE] = keys_ref[slot]
        out[CACHE : 2 * CACHE] = values_ref[slot]
        out[2 * CACHE :] = notes
    next(mig_x_steps)
    mig_sent = [mig_over(0)]
    straight = [send(mig_out.at[0], mig_in.at[0], ((r + 1) % REPLICAS, t))]
    for load in late_loads:
        load.wait()
    add_base(0)

    next(z_steps)
    next(y_steps)
    next(x_steps)
    next(mig_x_steps)
    tokens_sent += [tokens_over(1), tokens_over(NX - 1)]
    mig_sent += [mig_over(1), mig_over(NX - 1)]
    add_base(1)
    add_base(NY - 1)
    finish(x_steps)
    tokens_sent += [tokens_over(2)]
    finish(mig_x_steps)
    mig_sent += [mig_over(2)]

    next(z_steps)
    next(y_steps)
    next(near_steps)
    near_sent = [near_over(0)]

    for copy in mig_sent:
        copy.wait_recv()
    plane_offset, z_offset = other_offset % PLANE, other_offset // PLANE
    from_w = (w - plane_offset + PLANE) % PLANE
    carry = jnp.where(from_w + plane_offset >= PLANE, 1, 0)
    from_slot = (from_w // NC - x + NX) % NX * NC + (from_w % NC - c + NC) % NC
    mig_z[0] = mig_x[from_slot]

    for copy in tokens_sent:
        copy.wait_recv()
    lane = lanes((1, HD))
    stored_all = tok_x[:, :, PART:].reshape(PLANE * ROWS, HD).astype(F32)

    def add_products(pair, pairs):
        some = shrink_z[2 * pair : 2 * (pair + pairs)].reshape(2 * pairs * RANK, PART)
        product = lax.dot_general(
            tok_x[:, :, 0:PART].reshape(PLANE * ROWS, PART), some, (((1,), (1,)), ((), ())),
            preferred_element_type=F32,
        )
        out = None if pair == 0 else acc[...]
        for k in range(pairs):
            first, second = (
                ((r + d * PLANE) % REPLICAS).astype(F32) for d, at in SHRINK_AT.items() if at // 2 == pair + k
            )
            mine = stored_all == jnp.where(lane < RANK, first, second)
            term = jnp.where(mine, product[:, k * HD : (k + 1) * HD], 0.0)
            out = term if out is None else out + term
        return out

    acc[...] = add_products(0, 2)

    next(z_steps)
    next(y_steps)
    straight += [send(mig_out.at[1], mig_in.at[1], along_z(half // PLANE))]
    next(mig_steps)
    next(near_steps)
    near_sent += [near_over(1), near_over(NX - 1)]
    acc[...] = add_products(2, 1)
    add_base(2)
    add_base(NY - 2)
    next(mig_steps)
    next(z_steps)
    next(far_steps)
    far_sent = [far_over(0)]

    total = add_products(3, 1).reshape(PLANE, ROWS, HD)
    total = total + jnp.concatenate([total[:, :, RANK:], total[:, :, :RANK]], axis=-1)
    total = jnp.where(lanes((PLANE, HALF, HD)) < RANK, total[:, :HALF], total[:, HALF:])
    part_out[...] = total.astype(BF16)
    part_sent = []
    for dx in range(NX):
        for dc in range(NC):
            if dx or dc:
                back = (-dx % NX) * NC + dc
                part_sent.append(send(part_out.at[dx * NC + dc], part_x.at[back], in_plane(dx, dc)))
    part_x[0] = part_out[0]
    finish(near_steps)
    near_sent += [near_over(2)]
    next(far_steps)
    far_sent += [far_over(1), far_over(NX - 1)]
    for copy in part_sent:
        copy.wait_recv()
    part_y[0] = jnp.sum(part_x[...].astype(F32), axis=0).astype(BF16)
    over_y = [send(part_y.at[0], part_y.at[NY - d], along_y(d)) for d in range(1, NY)]
    add_base(3)
    add_base(NY - 3)
    next(y_steps)
    add_base(4)
    finish(far_steps)
    far_sent += [far_over(2)]
    next(mig_steps)
    next(mig_steps)
    next(mig_steps)
    from_z = (2 * NZ - z_offset - carry) % NZ
    arrived_ref[2] = mig_z[from_z]
    for k, copy in enumerate(straight):
        copy.wait_recv()
        arrived_ref[k] = mig_in[k]
    for copy in near_sent + far_sent:
        copy.wait_recv()
    expands = []
    for b in range(BLOCKS):
        oz, ow = stored[b] // PLANE, stored[b] % PLANE
        at = (ow // NC - x + NX) % NX * NC + (ow % NC - c + NC) % NC
        expands.append(expand_x[at, pick(EXPAND_AT, (oz - z + NZ) % NZ)])
    for copy in over_y:
        copy.wait_recv()
    shrink = jnp.sum(part_y[...].astype(F32), axis=0).astype(BF16)
    rows = ROWS // BLOCKS
    lane16 = lanes((rows, HD))
    deltas = [None] * BLOCKS
    for k in range(2):
        mine = shrink[k * rows : (k + 1) * rows].astype(F32)
        left = jnp.where(lane16 < RANK, mine, 0.0)
        right = jnp.where(lane16 < RANK, 0.0, mine)
        both = jnp.concatenate([expands[k], expands[k + 2]], axis=0)
        out = jnp.dot(jnp.concatenate([left, right], axis=0).astype(BF16), both, preferred_element_type=F32)
        deltas[k], deltas[k + 2] = out[:rows], out[rows:]
    fresh_ref[...] = (base + jnp.concatenate(deltas, axis=0)).astype(BF16)

    for copy in copies:
        copy.wait_send()


def attend_kernel(
    q_ref, draft_ref, keys_ref, values_ref, length_ref, arrived_ref, fresh_ref,
    out_hbm, ko_hbm, vo_hbm, out_ref, ko_ref, vo_ref, sem,
):
    group = q_ref.shape[2] // HD
    heads = group * STEPS
    spot = lax.broadcasted_iota(jnp.int32, (CACHE, HD), 0).astype(F32)
    landing = [arrived_ref[a, 2 * CACHE : 2 * CACHE + 1, :].astype(F32) for a in range(3)]
    lengths = [arrived_ref[a, 2 * CACHE + 1 : 2 * CACHE + 2, :].astype(F32) for a in range(3)]
    lane = lanes((1, HD))
    row_at = lax.broadcasted_iota(jnp.int32, (2 * heads, HD), 0)
    lane_at = lanes((2 * heads, HD))
    same = (row_at // heads) == (lane_at // CACHE)
    ahead = (lane_at % CACHE - row_at % STEPS).astype(F32)
    scale = 1.0 / math.sqrt(HD)
    pairs = range(SLOTS // 2)

    filled = []
    for s in range(SLOTS):
        fill = jnp.full((1, HD), length_ref[s].astype(F32))
        for a in range(3):
            fill = jnp.where(landing[a] == float(s), lengths[a], fill)
        filled.append(fill)

    def place(old_ref, first_row, new, out):
        for s in range(SLOTS):
            held = old_ref[s].astype(F32)
            for a in range(3):
                came = arrived_ref[a, first_row : first_row + CACHE].astype(F32)
                held = jnp.where(landing[a] == float(s), came, held)
            after = spot - filled[s]
            rows = new(s)
            for j in range(STEPS):
                held = jnp.where(after == float(j), rows[j : j + 1], held)
            out[s] = held.astype(BF16)

    place(keys_ref, 0, lambda s: draft_ref[s].astype(F32), ko_ref)
    keys_gone = pltpu.make_async_copy(ko_ref, ko_hbm, sem.at[0])
    keys_gone.start()
    scores = []
    for pair in pairs:
        queries = []
        for s in (2 * pair, 2 * pair + 1):
            query = q_ref[s].astype(F32)
            queries += [query[:, g * HD : (g + 1) * HD] for g in range(group)]
        stacked = jnp.concatenate(queries, axis=0).astype(BF16)
        both = ko_ref[2 * pair : 2 * pair + 2].reshape(2 * CACHE, HD)
        scores.append(lax.dot_general(stacked, both, (((1,), (1,)), ((), ())), preferred_element_type=F32) * scale)
    place(values_ref, CACHE, lambda s: fresh_ref[s * STEPS : (s + 1) * STEPS].astype(F32), vo_ref)
    values_gone = pltpu.make_async_copy(vo_ref, vo_hbm, sem.at[1])
    values_gone.start()
    weights = []
    for pair in pairs:
        allowed = same & (ahead <= jnp.where(lane < CACHE, filled[2 * pair], filled[2 * pair + 1]))
        masked = jnp.where(allowed, scores[pair], -1e30)
        top = jnp.max(masked, axis=-1, keepdims=True)
        raised = jnp.where(allowed, jnp.exp(masked - top), 0.0)
        weights.append((raised / jnp.sum(raised, axis=-1, keepdims=True)).astype(BF16))
    for pair in pairs:
        both = vo_ref[2 * pair : 2 * pair + 2].reshape(2 * CACHE, HD)
        attended = jnp.dot(weights[pair], both, preferred_element_type=F32)
        for k in range(2):
            for g in range(group):
                at = k * heads + g * STEPS
                out_ref[2 * pair + k, :, g * HD : (g + 1) * HD] = attended[at : at + STEPS].astype(BF16)
    out_gone = pltpu.make_async_copy(out_ref, out_hbm, sem.at[2])
    out_gone.start()
    keys_gone.wait()
    values_gone.wait()
    out_gone.wait()


def body(
    tokens,
    value_matrix,
    queries,
    draft_keys,
    key_cache_before,
    value_cache_before,
    cache_length,
    migrations,
    block_adapter_index,
    adapter_replica,
    adapter_shrink,
    adapter_expand,
):
    vmem = pl.BlockSpec(memory_space=pltpu.VMEM)
    hbm = pl.BlockSpec(memory_space=pltpu.HBM)
    smem = pl.BlockSpec(memory_space=pltpu.SMEM)
    fresh, arrived = pl.pallas_call(
        comm_kernel,
        out_shape=(
            jax.ShapeDtypeStruct((ROWS, HD), BF16),
            jax.ShapeDtypeStruct((3, MIG_ROWS, HD), BF16),
        ),
        in_specs=[hbm] * 10,
        out_specs=(vmem, vmem),
        scratch_shapes=[
            pltpu.VMEM(tokens.shape, BF16),
            pltpu.VMEM(value_matrix.shape, BF16),
            pltpu.VMEM(key_cache_before.shape, BF16),
            pltpu.VMEM(value_cache_before.shape, BF16),
            pltpu.SMEM(cache_length.shape, jnp.int32),
            pltpu.SMEM((3, 1, 3), jnp.int32),
            pltpu.SMEM(block_adapter_index.shape, jnp.int32),
            pltpu.SMEM(adapter_replica.shape, jnp.int32),
            pltpu.SemaphoreType.DMA((10,)),
            pltpu.VMEM((ROWS, PART), F32),
            pltpu.VMEM((NY, ROWS, PART), BF16),
            pltpu.VMEM((PLANE, ROWS, PART + HD), BF16),
            pltpu.VMEM((NZ, RANK, PART), BF16),
            pltpu.VMEM((PLANE, NZ, RANK, HD), BF16),
            pltpu.VMEM((2, MIG_ROWS, HD), BF16),
            pltpu.VMEM((2, MIG_ROWS, HD), BF16),
            pltpu.VMEM((PLANE, MIG_ROWS, HD), BF16),
            pltpu.VMEM((NZ, MIG_ROWS, HD), BF16),
            pltpu.VMEM((PLANE * ROWS, HD), F32),
            pltpu.VMEM((PLANE, HALF, HD), BF16),
            pltpu.VMEM((PLANE, HALF, HD), BF16),
            pltpu.VMEM((NY, HALF, HD), BF16),
            pltpu.SemaphoreType.DMA((COPIES,)),
            pltpu.SemaphoreType.DMA((COPIES,)),
        ],
        compiler_params=pltpu.CompilerParams(
            collective_id=0, has_side_effects=True, vmem_limit_bytes=32 * 1024 * 1024
        ),
        name="gather_and_project",
    )(
        *(
            pltpu.with_memory_space_constraint(operand, pltpu.HBM)
            for operand in (
                tokens,
                value_matrix,
                key_cache_before,
                value_cache_before,
                cache_length,
                jnp.transpose(migrations, (1, 0, 2)),
                block_adapter_index,
                adapter_replica,
                jnp.swapaxes(adapter_shrink[0], 0, 1),
                adapter_expand,
            )
        )
    )
    return pl.pallas_call(
        attend_kernel,
        out_shape=(
            jax.ShapeDtypeStruct(queries.shape, BF16),
            jax.ShapeDtypeStruct(key_cache_before.shape, BF16),
            jax.ShapeDtypeStruct(value_cache_before.shape, BF16),
        ),
        in_specs=[vmem, vmem, vmem, vmem, smem, vmem, vmem],
        out_specs=(hbm, hbm, hbm),
        scratch_shapes=[
            pltpu.VMEM(queries.shape, BF16),
            pltpu.VMEM(key_cache_before.shape, BF16),
            pltpu.VMEM(value_cache_before.shape, BF16),
            pltpu.SemaphoreType.DMA((3,)),
        ],
        compiler_params=pltpu.CompilerParams(vmem_limit_bytes=24 * 1024 * 1024),
        name="place_and_attend",
    )(queries, draft_keys, key_cache_before, value_cache_before, cache_length, arrived, fresh)


def solution(mesh):
    placed = (
        P("replica", None, "tensor"),
        P(None, "tensor"),
        P("replica", None, "tensor"),
        P("replica", None, "tensor"),
        P("replica", None, "tensor"),
        P("replica", None, "tensor"),
        P("replica"),
        P("replica", None, None),
        P("replica", None),
        P(),
        P("replica", "tensor", None),
        P("replica", None, "tensor"),
    )
    return jax.shard_map(
        body,
        mesh=mesh,
        in_specs=placed,
        out_specs=(
            P("replica", None, "tensor"),
            P("replica", None, "tensor"),
            P("replica", None, "tensor"),
        ),
        check_vma=False,
    )
```

time: 63.4 us -> 54.6 us (0.86)
  the two profiles are of different devices: /device:TPU:1 before, /device:TPU:4 now
where the time goes in v2:
time: 54.6 us; the launch traced here: 54.5 us
  Pallas kernels  53.8 us (99%)
  between operations  0.72 us (1%)
    pallas_call x1, Pallas kernels, body(): pl.pallas_call(comm_kernel, out_shape=(jax.ShapeDtypeStruct((ROWS, HD), B...  51.5 us
    pallas_call x1, Pallas kernels, body(): pl.pallas_call(attend_kernel, out_shape=(jax.ShapeDtypeStruct(queries.sha...  2.26 us

profile of v2, /device:TPU:4, one launch (start us, length us, event | category | flops | bytes accessed | tf_op | source)
XLA Modules:
  0.0 54.5 jit_solution(7533968248148049072)
XLA Ops:
  0.6 0.0 copy-start.4
  0.6 0.0 copy-start.1
  0.7 0.0 copy-start
  0.7 0.0 copy-start.3
  0.7 0.0 copy-start.2
  0.7 51.5 %gather_and_project.1 = (bf16[64,128]{1,0:T(8,128)(2,1)S(1)}, bf16[3,144,128]{2,1,0:T(8,128)(2,1)S(1)}) custom-call(bf16[16,4,1024]{2,1,0:T(4,128)(2,1)} %tok_hbm.1, bf16[8192,128]{1,0:T(8,128)(2,1)} %w_hbm.1, bf16[16,64,128]{2,1,0:T(8,128)(2,1)} %keys_ref.1, bf16[16,64,128]{2,1,0:T(8,128)(2,1)} %values_ref.1, s32[16]{0:T(128)} %length_ref.1, ...), custom_call_target="tpu_custom_call" | custom-call | tf_op jit(solution)/shard_map/gather_and_project/pallas_call | solution.py:447
  52.2 0.0 copy-done.4
  52.2 0.0 copy-done.1
  52.2 0.0 copy-done
  52.2 0.0 copy-done.3
  52.2 0.0 copy-done.2
  52.2 2.3 %place_and_attend.1 = (bf16[16,4,1024]{2,1,0:T(4,128)(2,1)}, bf16[16,64,128]{2,1,0:T(8,128)(2,1)}, bf16[16,64,128]{2,1,0:T(8,128)(2,1)}) custom-call(bf16[16,4,1024]{2,1,0:T(4,128)(2,1)S(1)} %copy-done.2, bf16[16,4,128]{2,1,0:T(4,128)(2,1)S(1)} %copy-done.3, bf16[16,64,128]{2,1,0:T(8,128)(2,1)S(1)} %copy-done, bf16[16,64,128]{2,1,0:T(8,128)(2,1)S(1)} %copy-done.1, ...), custom_call_target="tpu_custom_call" | custom-call | tf_op jit(solution)/shard_map/place_and_attend/pallas_call | solution.py:502
Async XLA Ops:
  0.6 51.5 %copy-start.4 = (s32[16]{0:T(128)S(1)}, s32[16]{0:T(128)}, u32[]{:S(2)}) copy-start(s32[16]{0:T(128)} %length_ref.1) | copy-start | bytes 196
  0.6 51.5 %copy-start.1 = (bf16[16,64,128]{2,1,0:T(8,128)(2,1)S(1)}, bf16[16,64,128]{2,1,0:T(8,128)(2,1)}, u32[]{:S(2)}) copy-start(bf16[16,64,128]{2,1,0:T(8,128)(2,1)} %values_ref.1) | copy-start | bytes 786436
  0.7 51.5 %copy-start = (bf16[16,64,128]{2,1,0:T(8,128)(2,1)S(1)}, bf16[16,64,128]{2,1,0:T(8,128)(2,1)}, u32[]{:S(2)}) copy-start(bf16[16,64,128]{2,1,0:T(8,128)(2,1)} %keys_ref.1) | copy-start | bytes 786436
  0.7 51.5 %copy-start.3 = (bf16[16,4,128]{2,1,0:T(4,128)(2,1)S(1)}, bf16[16,4,128]{2,1,0:T(4,128)(2,1)}, u32[]{:S(2)}) copy-start(bf16[16,4,128]{2,1,0:T(4,128)(2,1)} %draft_ref.1) | copy-start | bytes 49156
  0.7 51.5 %copy-start.2 = (bf16[16,4,1024]{2,1,0:T(4,128)(2,1)S(1)}, bf16[16,4,1024]{2,1,0:T(4,128)(2,1)}, u32[]{:S(2)}) copy-start(bf16[16,4,1024]{2,1,0:T(4,128)(2,1)} %q_ref.1) | copy-start | bytes 393220

commit v3 on v2

--- a/solution.py
+++ b/solution.py
@@ -1,3 +1,4 @@
+import itertools
 import math
 
 import jax
@@ -18,7 +19,7 @@
 PART = 1024
 HALF = ROWS // 2
 MIG_ROWS = 2 * CACHE + 16
-COPIES = 128
+COPIES = 136
 
 SHRINK_AT = {1: 0, 7: 1, 2: 2, 6: 3, 3: 4, 5: 5, 0: 6, 4: 7}
 EXPAND_AT = {1: 0, 7: 1, 2: 2, 6: 3, 0: 4, 3: 5, 5: 6, 4: 7}
@@ -58,10 +59,10 @@
         return (z * PLANE + ((x + dx) % NX) * NC + (c + dc) % NC, t)
 
     sibling = in_plane(0, 1)
-    copies = []
+    copies, numbers = [], itertools.count()
 
     def send(src, dst, device):
-        k = len(copies)
+        k = next(numbers)
         copy = pltpu.make_async_remote_copy(
             src_ref=src, dst_ref=dst, send_sem=send_sem.at[k], recv_sem=recv_sem.at[k],
             device_id=device, device_id_type=MESH,
@@ -93,34 +94,38 @@
             (w_hbm, w_ref),
         ])
     ]
+    load_w = loads.pop()
     for load in loads:
         load.start()
     tok_loads, mig_loads, late_loads = loads[:3], loads[3:7], loads[7:]
 
-    def ring(n, right, left, parts, split):
+    def ring(n, right, left, groups):
         gone = {}
         for k in range(1, n // 2 + 1):
-            stay = []
-            for h, (at, last) in enumerate(zip(parts, split)):
-                for way, device in ((-1, right), (1, left)):
-                    if k == n // 2 and last != way:
-                        stay.append(gone[k - 1, h, way])
-                        continue
-                    if k > 1:
-                        gone[k - 1, h, way].wait_recv()
-                    src, dst = way * (k - 1) % n, way * k % n
-                    gone[k, h, way] = send(at(src, k == 1), at(dst, False), device)
-            for copy in stay:
-                copy.wait_recv()
-            yield k - 1
-        for (k, _, _), copy in gone.items():
+            for h, views in enumerate(groups):
+                ways = {-1: right, 1: left}
+                stays = []
+                if k == n // 2:
+                    stays = [1 if 2 * h < len(groups) else -1]
+                    del ways[stays[0]]
+                for v, at in enumerate(views):
+                    for way, device in ways.items():
+                        if k > 1:
+                            gone[k - 1, h, v, way].wait_recv()
+                        src, dst = way * (k - 1) % n, way * k % n
+                        gone[k, h, v, way] = send(at(src, k == 1), at(dst, False), device)
+                for v in range(len(views)):
+                    for way in stays:
+                        gone[k - 1, h, v, way].wait_recv()
+                yield k, h
+        for (k, *_), copy in gone.items():
             if k == n // 2:
                 copy.wait_recv()
-        yield n // 2
-
-    def finish(steps):
-        for _ in steps:
-            pass
+        yield n, 0
+
+    def last(steps, n):
+        for _ in range(n):
+            next(steps)
 
     first_rows, last_rows = pl.ds(0, HALF), pl.ds(HALF, HALF)
 
@@ -130,40 +135,45 @@
     z_steps = ring(
         NZ, along_z(1), along_z(-1),
         [
-            lambda d, own: expand_hbm.at[0] if own else expand_x.at[0, EXPAND_AT[d]],
-            shrink_part(first_rows),
-            shrink_part(last_rows),
+            [lambda d, own: expand_hbm.at[0] if own else expand_x.at[0, EXPAND_AT[d]], shrink_part(pl.ds(0, 16))],
+            [shrink_part(pl.ds(16, 16))],
+            [shrink_part(pl.ds(32, 16))],
+            [shrink_part(pl.ds(48, 16))],
         ],
-        [-1, -1, 1],
     )
     y_steps = ring(
         NY, along_y(1), along_y(-1),
-        [lambda d, own: tok_y.at[d, first_rows], lambda d, own: tok_y.at[d, last_rows]],
-        [-1, 1],
-    )
-
-    def x_ring(parts):
-        return ring(NX, in_plane(1, 0), in_plane(-1, 0), parts, [-1, 1])
+        [[lambda d, own: tok_y.at[d, first_rows]], [lambda d, own: tok_y.at[d, last_rows]]],
+    )
+
+    def x_ring(first, second):
+        return ring(NX, in_plane(1, 0), in_plane(-1, 0), [[first], [second]])
 
     x_steps = x_ring(
-        [lambda d, own: tok_x.at[d * NC, first_rows], lambda d, own: tok_x.at[d * NC, last_rows]]
+        lambda d, own: tok_x.at[d * NC, first_rows], lambda d, own: tok_x.at[d * NC, last_rows]
     )
     mig_halves = pl.ds(0, CACHE), pl.ds(CACHE, MIG_ROWS - CACHE)
     mig_x_steps = x_ring(
-        [lambda d, own: mig_x.at[d * NC, mig_halves[0]], lambda d, own: mig_x.at[d * NC, mig_halves[1]]]
+        lambda d, own: mig_x.at[d * NC, mig_halves[0]], lambda d, own: mig_x.at[d * NC, mig_halves[1]]
     )
     mig_steps = ring(
         NZ, along_z(1), along_z(-1),
-        [lambda d, own: mig_z.at[d, mig_halves[0]], lambda d, own: mig_z.at[d, mig_halves[1]]],
-        [-1, 1],
-    )
-
-    def expand_ring(first, middle, last):
-        early, late = pl.ds(first, middle - first), pl.ds(middle, last - middle)
-        return x_ring([lambda d, own: expand_x.at[d * NC, early], lambda d, own: expand_x.at[d * NC, late]])
+        [[lambda d, own: mig_z.at[d, mig_halves[0]]], [lambda d, own: mig_z.at[d, mig_halves[1]]]],
+    )
+
+    def expand_ring(first, middle, end):
+        early, late = pl.ds(first, middle - first), pl.ds(middle, end - middle)
+        return x_ring(lambda d, own: expand_x.at[d * NC, early], lambda d, own: expand_x.at[d * NC, late])
 
     near_steps = expand_ring(0, 3, NEAR)
-    far_steps = expand_ring(NEAR, NZ - 1, NZ)
+
+    def to_plane(src, dst):
+        return [
+            send(src(dx * NC + dc), dst((-dx % NX) * NC + dc), in_plane(dx, dc))
+            for dx in range(NX)
+            for dc in range(NC)
+            if dx or dc
+        ]
 
     def to_sibling(at):
         return lambda d: send(at(d * NC), at(d * NC + 1), sibling)
@@ -171,7 +181,6 @@
     tokens_over = to_sibling(lambda at: tok_x.at[at])
     mig_over = to_sibling(lambda at: mig_x.at[at])
     near_over = to_sibling(lambda at: expand_x.at[at, pl.ds(0, NEAR)])
-    far_over = to_sibling(lambda at: expand_x.at[at, pl.ds(NEAR, NZ - NEAR)])
 
     base = None
 
@@ -182,15 +191,13 @@
         base = term if base is None else base + term
 
     pl.semaphore_wait(barrier, len(others))
-    next(z_steps)
+    last(z_steps, 4)
 
     for load in tok_loads:
         load.wait()
     for s in range(SLOTS):
         tok_f32[s * STEPS : (s + 1) * STEPS, :] = tok_ref[s].astype(F32)
     own = tok_f32[...].astype(BF16)
-    tok_y[0] = own
-    next(y_steps)
     tok_x[0, :, 0:PART] = own
     row = lax.broadcasted_iota(jnp.int32, (ROWS, HD), 0)
     stored = [owner_ref[index_ref[0, b]] for b in range(BLOCKS)]
@@ -198,8 +205,11 @@
     for b in range(BLOCKS):
         stored_rows = jnp.where(row // (ROWS // BLOCKS) == b, stored[b].astype(F32), stored_rows)
     tok_x[0, :, PART:] = stored_rows.astype(BF16)
-    next(x_steps)
+    last(x_steps, 2)
     tokens_sent = [tokens_over(0)]
+    tok_y[0] = own
+    last(y_steps, 2)
+    load_w.start()
 
     for load in mig_loads:
         load.wait()
@@ -226,43 +236,29 @@
         out[0:CACHE] = keys_ref[slot]
         out[CACHE : 2 * CACHE] = values_ref[slot]
         out[2 * CACHE :] = notes
-    next(mig_x_steps)
+    last(mig_x_steps, 2)
     mig_sent = [mig_over(0)]
     straight = [send(mig_out.at[0], mig_in.at[0], ((r + 1) % REPLICAS, t))]
     for load in late_loads:
         load.wait()
+    load_w.wait()
     add_base(0)
-
-    next(z_steps)
-    next(y_steps)
-    next(x_steps)
-    next(mig_x_steps)
+    last(z_steps, 4)
+    last(x_steps, 2)
     tokens_sent += [tokens_over(1), tokens_over(NX - 1)]
+    last(mig_x_steps, 2)
     mig_sent += [mig_over(1), mig_over(NX - 1)]
-    add_base(1)
-    add_base(NY - 1)
-    finish(x_steps)
+    last(z_steps, 4)
+    last(x_steps, 1)
     tokens_sent += [tokens_over(2)]
-    finish(mig_x_steps)
+    last(mig_x_steps, 1)
     mig_sent += [mig_over(2)]
-
-    next(z_steps)
-    next(y_steps)
-    next(near_steps)
+    last(near_steps, 2)
     near_sent = [near_over(0)]
-
-    for copy in mig_sent:
-        copy.wait_recv()
-    plane_offset, z_offset = other_offset % PLANE, other_offset // PLANE
-    from_w = (w - plane_offset + PLANE) % PLANE
-    carry = jnp.where(from_w + plane_offset >= PLANE, 1, 0)
-    from_slot = (from_w // NC - x + NX) % NX * NC + (from_w % NC - c + NC) % NC
-    mig_z[0] = mig_x[from_slot]
-
+    last(y_steps, 2)
     for copy in tokens_sent:
         copy.wait_recv()
     lane = lanes((1, HD))
-    stored_all = tok_x[:, :, PART:].reshape(PLANE * ROWS, HD).astype(F32)
 
     def add_products(pair, pairs):
         some = shrink_z[2 * pair : 2 * (pair + pairs)].reshape(2 * pairs * RANK, PART)
@@ -270,6 +266,7 @@
             tok_x[:, :, 0:PART].reshape(PLANE * ROWS, PART), some, (((1,), (1,)), ((), ())),
             preferred_element_type=F32,
         )
+        stored_all = tok_x[:, :, PART:].reshape(PLANE * ROWS, HD).astype(F32)
         out = None if pair == 0 else acc[...]
         for k in range(pairs):
             first, second = (
@@ -282,48 +279,50 @@
 
     acc[...] = add_products(0, 2)
 
-    next(z_steps)
-    next(y_steps)
-    straight += [send(mig_out.at[1], mig_in.at[1], along_z(half // PLANE))]
-    next(mig_steps)
-    next(near_steps)
+    last(z_steps, 4)
+    far = pl.ds(NEAR, 2)
+    far_sent = to_plane(lambda at: expand_x.at[0, far], lambda at: expand_x.at[at, far])
+    for copy in mig_sent:
+        copy.wait_recv()
+    plane_offset, z_offset = other_offset % PLANE, other_offset // PLANE
+    from_w = (w - plane_offset + PLANE) % PLANE
+    carry = jnp.where(from_w + plane_offset >= PLANE, 1, 0)
+    from_slot = (from_w // NC - x + NX) % NX * NC + (from_w % NC - c + NC) % NC
+    mig_z[0] = mig_x[from_slot]
+    last(mig_steps, 2)
+    last(near_steps, 2)
     near_sent += [near_over(1), near_over(NX - 1)]
     acc[...] = add_products(2, 1)
-    add_base(2)
-    add_base(NY - 2)
-    next(mig_steps)
-    next(z_steps)
-    next(far_steps)
-    far_sent = [far_over(0)]
+    last(z_steps, 1)
+    far_sent += to_plane(lambda at: expand_x.at[0, NZ - 1], lambda at: expand_x.at[at, NZ - 1])
+    last(mig_steps, 2)
 
     total = add_products(3, 1).reshape(PLANE, ROWS, HD)
     total = total + jnp.concatenate([total[:, :, RANK:], total[:, :, :RANK]], axis=-1)
     total = jnp.where(lanes((PLANE, HALF, HD)) < RANK, total[:, :HALF], total[:, HALF:])
     part_out[...] = total.astype(BF16)
-    part_sent = []
-    for dx in range(NX):
-        for dc in range(NC):
-            if dx or dc:
-                back = (-dx % NX) * NC + dc
-                part_sent.append(send(part_out.at[dx * NC + dc], part_x.at[back], in_plane(dx, dc)))
+    part_sent = to_plane(lambda at: part_out.at[at], lambda at: part_x.at[at])
     part_x[0] = part_out[0]
-    finish(near_steps)
+    straight += [send(mig_out.at[1], mig_in.at[1], along_z(half // PLANE))]
+    last(near_steps, 1)
     near_sent += [near_over(2)]
-    next(far_steps)
-    far_sent += [far_over(1), far_over(NX - 1)]
+    last(y_steps, 2)
+    add_base(1)
+    add_base(NY - 1)
+    last(mig_steps, 2)
     for copy in part_sent:
         copy.wait_recv()
     part_y[0] = jnp.sum(part_x[...].astype(F32), axis=0).astype(BF16)
     over_y = [send(part_y.at[0], part_y.at[NY - d], along_y(d)) for d in range(1, NY)]
+    last(y_steps, 2)
+    last(mig_steps, 2)
+    add_base(2)
+    add_base(NY - 2)
     add_base(3)
     add_base(NY - 3)
-    next(y_steps)
+    last(y_steps, 1)
     add_base(4)
-    finish(far_steps)
-    far_sent += [far_over(2)]
-    next(mig_steps)
-    next(mig_steps)
-    next(mig_steps)
+    last(mig_steps, 1)
     from_z = (2 * NZ - z_offset - carry) % NZ
     arrived_ref[2] = mig_z[from_z]
     for k, copy in enumerate(straight):

time: 54.6 us -> 48.2 us (0.88)
  the two profiles are of different devices: /device:TPU:4 before, /device:TPU:1 now
where the time goes in v3:
time: 48.2 us; the launch traced here: 48.1 us
  Pallas kernels  47.4 us (98%)
  between operations  0.72 us (1%)
    pallas_call x1, Pallas kernels, body(): pl.pallas_call(comm_kernel, out_shape=(jax.ShapeDtypeStruct((ROWS, HD), B...  45.1 us
    pallas_call x1, Pallas kernels, body(): pl.pallas_call(attend_kernel, out_shape=(jax.ShapeDtypeStruct(queries.sha...  2.26 us

profile of v3, /device:TPU:1, one launch (start us, length us, event | category | flops | bytes accessed | tf_op | source)
XLA Modules:
  0.0 48.1 jit_solution(17057079930454771968)
XLA Ops:
  0.6 0.0 copy-start.4
  0.6 0.0 copy-start.1
  0.7 0.0 copy-start
  0.7 0.0 copy-start.3
  0.7 0.0 copy-start.2
  0.7 45.1 %gather_and_project.1 = (bf16[64,128]{1,0:T(8,128)(2,1)S(1)}, bf16[3,144,128]{2,1,0:T(8,128)(2,1)S(1)}) custom-call(bf16[16,4,1024]{2,1,0:T(4,128)(2,1)} %tok_hbm.1, bf16[8192,128]{1,0:T(8,128)(2,1)} %w_hbm.1, bf16[16,64,128]{2,1,0:T(8,128)(2,1)} %keys_ref.1, bf16[16,64,128]{2,1,0:T(8,128)(2,1)} %values_ref.1, s32[16]{0:T(128)} %length_ref.1, ...), custom_call_target="tpu_custom_call" | custom-call | tf_op jit(solution)/shard_map/gather_and_project/pallas_call | solution.py:446
  45.8 0.0 copy-done.4
  45.8 0.0 copy-done.1
  45.8 0.0 copy-done
  45.8 0.0 copy-done.3
  45.8 0.0 copy-done.2
  45.8 2.3 %place_and_attend.1 = (bf16[16,4,1024]{2,1,0:T(4,128)(2,1)}, bf16[16,64,128]{2,1,0:T(8,128)(2,1)}, bf16[16,64,128]{2,1,0:T(8,128)(2,1)}) custom-call(bf16[16,4,1024]{2,1,0:T(4,128)(2,1)S(1)} %copy-done.2, bf16[16,4,128]{2,1,0:T(4,128)(2,1)S(1)} %copy-done.3, bf16[16,64,128]{2,1,0:T(8,128)(2,1)S(1)} %copy-done, bf16[16,64,128]{2,1,0:T(8,128)(2,1)S(1)} %copy-done.1, ...), custom_call_target="tpu_custom_call" | custom-call | tf_op jit(solution)/shard_map/place_and_attend/pallas_call | solution.py:501
Async XLA Ops:
  0.6 45.1 %copy-start.4 = (s32[16]{0:T(128)S(1)}, s32[16]{0:T(128)}, u32[]{:S(2)}) copy-start(s32[16]{0:T(128)} %length_ref.1) | copy-start | bytes 196
  0.6 45.1 %copy-start.1 = (bf16[16,64,128]{2,1,0:T(8,128)(2,1)S(1)}, bf16[16,64,128]{2,1,0:T(8,128)(2,1)}, u32[]{:S(2)}) copy-start(bf16[16,64,128]{2,1,0:T(8,128)(2,1)} %values_ref.1) | copy-start | bytes 786436
  0.7 45.1 %copy-start = (bf16[16,64,128]{2,1,0:T(8,128)(2,1)S(1)}, bf16[16,64,128]{2,1,0:T(8,128)(2,1)}, u32[]{:S(2)}) copy-start(bf16[16,64,128]{2,1,0:T(8,128)(2,1)} %keys_ref.1) | copy-start | bytes 786436
  0.7 45.1 %copy-start.3 = (bf16[16,4,128]{2,1,0:T(4,128)(2,1)S(1)}, bf16[16,4,128]{2,1,0:T(4,128)(2,1)}, u32[]{:S(2)}) copy-start(bf16[16,4,128]{2,1,0:T(4,128)(2,1)} %draft_ref.1) | copy-start | bytes 49156
  0.7 45.1 %copy-start.2 = (bf16[16,4,1024]{2,1,0:T(4,128)(2,1)S(1)}, bf16[16,4,1024]{2,1,0:T(4,128)(2,1)}, u32[]{:S(2)}) copy-start(bf16[16,4,1024]{2,1,0:T(4,128)(2,1)} %q_ref.1) | copy-start | bytes 393220

commit v4 on v2

--- a/solution.py
+++ b/solution.py
@@ -1,3 +1,4 @@
+import itertools
 import math
 
 import jax
@@ -18,11 +19,14 @@
 PART = 1024
 HALF = ROWS // 2
 MIG_ROWS = 2 * CACHE + 16
-COPIES = 128
-
-SHRINK_AT = {1: 0, 7: 1, 2: 2, 6: 3, 3: 4, 5: 5, 0: 6, 4: 7}
-EXPAND_AT = {1: 0, 7: 1, 2: 2, 6: 3, 0: 4, 3: 5, 5: 6, 4: 7}
-NEAR = 5
+COPIES = 80
+
+WIDE = PART + HD
+MIG_TILES = MIG_ROWS // 16
+
+ADAPTER_AT = {1: 0, 7: 1, 2: 2, 6: 3, 0: 4, 3: 5, 5: 6, 4: 7}
+OWN, NEAR = 4, 5
+X_AT = {0: 0, 1: 1, 2: 3, 3: 2}
 
 
 def pick(table, index):
@@ -41,7 +45,7 @@
     tok_hbm, w_hbm, keys_hbm, values_hbm, length_hbm, mig_hbm, index_hbm, owner_hbm, shrink_hbm, expand_hbm,
     fresh_ref, arrived_ref,
     tok_ref, w_ref, keys_ref, values_ref, length_ref, mig_ref, index_ref, owner_ref, load_sem, tok_f32,
-    tok_y, tok_x, shrink_z, expand_x, mig_out, mig_in, mig_x, mig_z,
+    tok_y, tok_x, adapter_z, expand_x, mig_out, mig_in, mig_z,
     acc, part_out, part_x, part_y, send_sem, recv_sem,
 ):
     r, t = lax.axis_index("replica"), lax.axis_index("tensor")
@@ -58,10 +62,10 @@
         return (z * PLANE + ((x + dx) % NX) * NC + (c + dc) % NC, t)
 
     sibling = in_plane(0, 1)
-    copies = []
+    copies, numbers = [], itertools.count()
 
     def send(src, dst, device):
-        k = len(copies)
+        k = next(numbers)
         copy = pltpu.make_async_remote_copy(
             src_ref=src, dst_ref=dst, send_sem=send_sem.at[k], recv_sem=recv_sem.at[k],
             device_id=device, device_id_type=MESH,
@@ -70,17 +74,16 @@
         copy.start()
         return copy
 
-    barrier = pltpu.get_barrier_semaphore()
-    others = [along_z(1), along_z(-1), along_z(NZ // 2)]
-    others += [along_y(d) for d in range(1, NY)]
-    others += [in_plane(dx, dc) for dx in range(NX) for dc in range(NC) if dx or dc]
-    others += [((r + 1) % REPLICAS, t), ((r + REPLICAS - 1) % REPLICAS, t)]
-    for other in others:
-        pl.semaphore_signal(barrier, inc=1, device_id=other, device_id_type=MESH)
+    def plane_at(dx, dc):
+        return dc * NX + X_AT[dx % NX]
+
+    far_first = [(dx, dc) for dx in (2, 1, 3, 0) for dc in range(NC) if dx or dc]
 
     loads = [
         pltpu.make_async_copy(src, dst, load_sem.at[k])
         for k, (src, dst) in enumerate([
+            (shrink_hbm, adapter_z.at[OWN, :, pl.ds(0, PART)]),
+            (expand_hbm.at[0], adapter_z.at[OWN, :, pl.ds(PART, HD)]),
             (tok_hbm, tok_ref),
             (index_hbm, index_ref),
             (owner_hbm, owner_ref),
@@ -88,90 +91,83 @@
             (length_hbm, length_ref),
             (keys_hbm, keys_ref),
             (values_hbm, values_ref),
-            (shrink_hbm, shrink_z.at[SHRINK_AT[0]]),
-            (expand_hbm.at[0], expand_x.at[0, EXPAND_AT[0]]),
             (w_hbm, w_ref),
         ])
     ]
+    load_w = loads.pop()
     for load in loads:
         load.start()
-    tok_loads, mig_loads, late_loads = loads[:3], loads[3:7], loads[7:]
-
-    def ring(n, right, left, parts, split):
-        gone = {}
-        for k in range(1, n // 2 + 1):
-            stay = []
-            for h, (at, last) in enumerate(zip(parts, split)):
-                for way, device in ((-1, right), (1, left)):
-                    if k == n // 2 and last != way:
-                        stay.append(gone[k - 1, h, way])
-                        continue
+
+    barrier = pltpu.get_barrier_semaphore()
+    others = [along_z(d) for d in (1, -1, 2, -2, NZ // 2)]
+    others += [along_y(d) for d in range(1, NY)]
+    others += [in_plane(dx, dc) for dx, dc in far_first]
+    others += [((r + 1) % REPLICAS, t), ((r + REPLICAS - 1) % REPLICAS, t)]
+    for other in others:
+        pl.semaphore_signal(barrier, inc=1, device_id=other, device_id_type=MESH)
+
+    def ring_of_8(to, views, halves):
+        gone, last = {}, []
+        for k in (1, 2, 3):
+            for h, at in enumerate(views):
+                for way in (-1, 1):
                     if k > 1:
-                        gone[k - 1, h, way].wait_recv()
-                    src, dst = way * (k - 1) % n, way * k % n
-                    gone[k, h, way] = send(at(src, k == 1), at(dst, False), device)
-            for copy in stay:
-                copy.wait_recv()
-            yield k - 1
-        for (k, _, _), copy in gone.items():
-            if k == n // 2:
-                copy.wait_recv()
-        yield n // 2
-
-    def finish(steps):
-        for _ in steps:
-            pass
-
-    first_rows, last_rows = pl.ds(0, HALF), pl.ds(HALF, HALF)
-
-    def shrink_part(rows):
-        return lambda d, own: shrink_hbm.at[rows] if own else shrink_z.at[SHRINK_AT[d], rows]
-
-    z_steps = ring(
-        NZ, along_z(1), along_z(-1),
-        [
-            lambda d, own: expand_hbm.at[0] if own else expand_x.at[0, EXPAND_AT[d]],
-            shrink_part(first_rows),
-            shrink_part(last_rows),
-        ],
-        [-1, -1, 1],
+                        gone[h, way].wait_recv()
+                    gone[h, way] = send(at(way * (k - 1) % 8), at(way * k % 8), to(-way))
+                if k == 3 and len(views) == 4:
+                    way = (-1, -1, 1, 1)[h]
+                    last.append(send(at(way * 2 % 8), at(4), to(-2 * way)))
+            if k == 3 and len(views) == 1:
+                last += [send(at(way * 2 % 8), at(4), to(-2 * way)) for way, at in zip((-1, 1), halves)]
+            yield
+        for copy in list(gone.values()):
+            copy.wait_recv()
+        yield
+        for copy in last:
+            copy.wait_recv()
+        yield
+
+    def ring_of_4(to, whole, halves):
+        gone = {way: send(whole(0), whole(way % 4), to(-way)) for way in (-1, 1)}
+        yield
+        for copy in gone.values():
+            copy.wait_recv()
+        gone = [send(at(way % 4), at(2), to(-way)) for way, at in zip((-1, 1), halves)]
+        yield
+        for copy in gone:
+            copy.wait_recv()
+        yield
+
+    def quarter(k):
+        return lambda d: adapter_z.at[ADAPTER_AT[d], pl.ds(16 * k, 16)]
+
+    z_steps = ring_of_8(along_z, [quarter(k) for k in range(4)], None)
+    y_steps = ring_of_8(
+        along_y,
+        [lambda d: tok_y.at[d]],
+        [lambda d: tok_y.at[d, pl.ds(0, HALF)], lambda d: tok_y.at[d, pl.ds(HALF, HALF)]],
     )
-    y_steps = ring(
-        NY, along_y(1), along_y(-1),
-        [lambda d, own: tok_y.at[d, first_rows], lambda d, own: tok_y.at[d, last_rows]],
-        [-1, 1],
+    x_steps = ring_of_4(
+        lambda d: in_plane(d, 0),
+        lambda d: tok_x.at[X_AT[d]],
+        [lambda d: tok_x.at[X_AT[d], pl.ds(0, HALF)], lambda d: tok_x.at[X_AT[d], pl.ds(HALF, HALF + 16)]],
     )
-
-    def x_ring(parts):
-        return ring(NX, in_plane(1, 0), in_plane(-1, 0), parts, [-1, 1])
-
-    x_steps = x_ring(
-        [lambda d, own: tok_x.at[d * NC, first_rows], lambda d, own: tok_x.at[d * NC, last_rows]]
+    mig_steps = ring_of_8(
+        along_z,
+        [lambda d: mig_z.at[d]],
+        [lambda d: mig_z.at[d, pl.ds(0, CACHE)], lambda d: mig_z.at[d, pl.ds(CACHE, MIG_ROWS - CACHE)]],
     )
-    mig_halves = pl.ds(0, CACHE), pl.ds(CACHE, MIG_ROWS - CACHE)
-    mig_x_steps = x_ring(
-        [lambda d, own: mig_x.at[d * NC, mig_halves[0]], lambda d, own: mig_x.at[d * NC, mig_halves[1]]]
-    )
-    mig_steps = ring(
-        NZ, along_z(1), along_z(-1),
-        [lambda d, own: mig_z.at[d, mig_halves[0]], lambda d, own: mig_z.at[d, mig_halves[1]]],
-        [-1, 1],
-    )
-
-    def expand_ring(first, middle, last):
-        early, late = pl.ds(first, middle - first), pl.ds(middle, last - middle)
-        return x_ring([lambda d, own: expand_x.at[d * NC, early], lambda d, own: expand_x.at[d * NC, late]])
-
-    near_steps = expand_ring(0, 3, NEAR)
-    far_steps = expand_ring(NEAR, NZ - 1, NZ)
-
-    def to_sibling(at):
-        return lambda d: send(at(d * NC), at(d * NC + 1), sibling)
-
-    tokens_over = to_sibling(lambda at: tok_x.at[at])
-    mig_over = to_sibling(lambda at: mig_x.at[at])
-    near_over = to_sibling(lambda at: expand_x.at[at, pl.ds(0, NEAR)])
-    far_over = to_sibling(lambda at: expand_x.at[at, pl.ds(NEAR, NZ - NEAR)])
+
+    def to_plane(src, dst):
+        return [send(src(plane_at(dx, dc)), dst(plane_at(-dx, dc)), in_plane(dx, dc)) for dx, dc in far_first]
+
+    def expands_along_x(some):
+        return [
+            send(expand_x.at[0, some], expand_x.at[plane_at(-dx, 0), some], in_plane(dx, 0)) for dx in (2, 1, 3)
+        ]
+
+    def expands_over(some):
+        return send(expand_x.at[pl.ds(0, NX), some], expand_x.at[pl.ds(NX, NX), some], sibling)
 
     base = None
 
@@ -181,28 +177,24 @@
         term = jnp.dot(tok_y[d], w_ref[pl.ds(rows, PART), :], preferred_element_type=F32)
         base = term if base is None else base + term
 
+    for load in loads[:2]:
+        load.wait()
     pl.semaphore_wait(barrier, len(others))
     next(z_steps)
 
-    for load in tok_loads:
+    for load in loads[2:]:
         load.wait()
     for s in range(SLOTS):
         tok_f32[s * STEPS : (s + 1) * STEPS, :] = tok_ref[s].astype(F32)
     own = tok_f32[...].astype(BF16)
-    tok_y[0] = own
-    next(y_steps)
-    tok_x[0, :, 0:PART] = own
+    tok_x[0, 0:ROWS, 0:PART] = own
     row = lax.broadcasted_iota(jnp.int32, (ROWS, HD), 0)
     stored = [owner_ref[index_ref[0, b]] for b in range(BLOCKS)]
     stored_rows = jnp.zeros((ROWS, HD), F32)
     for b in range(BLOCKS):
         stored_rows = jnp.where(row // (ROWS // BLOCKS) == b, stored[b].astype(F32), stored_rows)
-    tok_x[0, :, PART:] = stored_rows.astype(BF16)
-    next(x_steps)
-    tokens_sent = [tokens_over(0)]
-
-    for load in mig_loads:
-        load.wait()
+    tok_x[0, 0:ROWS, PART:] = stored_rows.astype(BF16)
+
     offsets = [(mig_ref[e, 0, 1] - r + REPLICAS) % REPLICAS for e in range(3)]
     half = REPLICAS // 2
     fits = [
@@ -215,65 +207,65 @@
         first, second, third = (column(e) for e in range(3))
         return jnp.where(fits[which][0], first, jnp.where(fits[which][1], second, third))
 
-    other_offset = chosen(2, lambda e: offsets[e])
-    mig_row = lax.broadcasted_iota(jnp.int32, (16, HD), 0)
-    for which in range(3):
+    def leaving(which):
         slot = chosen(which, lambda e: mig_ref[e, 0, 0])
         landing = chosen(which, lambda e: mig_ref[e, 0, 2]).astype(F32)
         filled = length_ref[slot].astype(F32)
-        notes = jnp.where(mig_row == 0, landing, filled).astype(BF16)
-        out = mig_x.at[0] if which == 2 else mig_out.at[which]
-        out[0:CACHE] = keys_ref[slot]
-        out[CACHE : 2 * CACHE] = values_ref[slot]
-        out[2 * CACHE :] = notes
-    next(mig_x_steps)
-    mig_sent = [mig_over(0)]
+        notes = jnp.where(lax.broadcasted_iota(jnp.int32, (16, HD), 0) == 0, landing, filled)
+        return jnp.concatenate([keys_ref[slot], values_ref[slot], notes.astype(BF16)], axis=0)
+
+    other = leaving(2)
+    for k in range(MIG_TILES):
+        tok_x[0, ROWS:, k * HD : (k + 1) * HD] = other[k * 16 : (k + 1) * 16]
+    next(x_steps)
+    tok_y[0] = own
+    next(y_steps)
+    load_w.start()
+    for which in range(2):
+        mig_out[which] = leaving(which)
     straight = [send(mig_out.at[0], mig_in.at[0], ((r + 1) % REPLICAS, t))]
-    for load in late_loads:
-        load.wait()
+    load_w.wait()
     add_base(0)
-
     next(z_steps)
+    next(x_steps)
+    tokens_over = [send(tok_x.at[pl.ds(0, 3)], tok_x.at[pl.ds(NX, 3)], sibling)]
     next(y_steps)
-    next(x_steps)
-    next(mig_x_steps)
-    tokens_sent += [tokens_over(1), tokens_over(NX - 1)]
-    mig_sent += [mig_over(1), mig_over(NX - 1)]
     add_base(1)
     add_base(NY - 1)
-    finish(x_steps)
-    tokens_sent += [tokens_over(2)]
-    finish(mig_x_steps)
-    mig_sent += [mig_over(2)]
-
     next(z_steps)
+    next(x_steps)
+    tokens_over += [send(tok_x.at[3], tok_x.at[NX + 3], sibling)]
+    near, far = pl.ds(0, NEAR), pl.ds(NEAR, NZ - NEAR)
+    expand_x[0, 0:NEAR] = adapter_z[0:NEAR, :, PART:]
+    near_sent = expands_along_x(near)
     next(y_steps)
-    next(near_steps)
-    near_sent = [near_over(0)]
-
-    for copy in mig_sent:
-        copy.wait_recv()
+    for copy in tokens_over:
+        copy.wait_recv()
+    other_offset = chosen(2, lambda e: offsets[e])
     plane_offset, z_offset = other_offset % PLANE, other_offset // PLANE
     from_w = (w - plane_offset + PLANE) % PLANE
     carry = jnp.where(from_w + plane_offset >= PLANE, 1, 0)
-    from_slot = (from_w // NC - x + NX) % NX * NC + (from_w % NC - c + NC) % NC
-    mig_z[0] = mig_x[from_slot]
-
-    for copy in tokens_sent:
-        copy.wait_recv()
+
+    def plane_slot(place):
+        return (place % NC - c + NC) % NC * NX + pick(X_AT, (place // NC - x + NX) % NX)
+
+    from_slot = plane_slot(from_w)
+    for k in range(MIG_TILES):
+        mig_z[0, k * 16 : (k + 1) * 16] = tok_x[from_slot, ROWS:, k * HD : (k + 1) * HD]
+    next(mig_steps)
     lane = lanes((1, HD))
-    stored_all = tok_x[:, :, PART:].reshape(PLANE * ROWS, HD).astype(F32)
 
     def add_products(pair, pairs):
-        some = shrink_z[2 * pair : 2 * (pair + pairs)].reshape(2 * pairs * RANK, PART)
+        some = adapter_z[2 * pair : 2 * (pair + pairs), :, 0:PART].reshape(2 * pairs * RANK, PART)
         product = lax.dot_general(
-            tok_x[:, :, 0:PART].reshape(PLANE * ROWS, PART), some, (((1,), (1,)), ((), ())),
+            tok_x[:, 0:ROWS, 0:PART].reshape(PLANE * ROWS, PART), some, (((1,), (1,)), ((), ())),
             preferred_element_type=F32,
         )
+        stored_all = tok_x[:, 0:ROWS, PART:].reshape(PLANE * ROWS, HD).astype(F32)
         out = None if pair == 0 else acc[...]
         for k in range(pairs):
             first, second = (
-                ((r + d * PLANE) % REPLICAS).astype(F32) for d, at in SHRINK_AT.items() if at // 2 == pair + k
+                ((r + d * PLANE) % REPLICAS).astype(F32) for d, at in ADAPTER_AT.items() if at // 2 == pair + k
             )
             mine = stored_all == jnp.where(lane < RANK, first, second)
             term = jnp.where(mine, product[:, k * HD : (k + 1) * HD], 0.0)
@@ -283,59 +275,53 @@
     acc[...] = add_products(0, 2)
 
     next(z_steps)
+    for copy in near_sent:
+        copy.wait_recv()
+    expand_over = [expands_over(near)]
     next(y_steps)
-    straight += [send(mig_out.at[1], mig_in.at[1], along_z(half // PLANE))]
     next(mig_steps)
-    next(near_steps)
-    near_sent += [near_over(1), near_over(NX - 1)]
-    acc[...] = add_products(2, 1)
     add_base(2)
     add_base(NY - 2)
-    next(mig_steps)
+    acc[...] = add_products(2, 1)
     next(z_steps)
-    next(far_steps)
-    far_sent = [far_over(0)]
 
     total = add_products(3, 1).reshape(PLANE, ROWS, HD)
     total = total + jnp.concatenate([total[:, :, RANK:], total[:, :, :RANK]], axis=-1)
     total = jnp.where(lanes((PLANE, HALF, HD)) < RANK, total[:, :HALF], total[:, HALF:])
     part_out[...] = total.astype(BF16)
-    part_sent = []
-    for dx in range(NX):
-        for dc in range(NC):
-            if dx or dc:
-                back = (-dx % NX) * NC + dc
-                part_sent.append(send(part_out.at[dx * NC + dc], part_x.at[back], in_plane(dx, dc)))
+    part_sent = to_plane(lambda at: part_out.at[at], lambda at: part_x.at[at])
+    expand_x[0, NEAR:] = adapter_z[NEAR:, :, PART:]
+    far_sent = expands_along_x(far)
     part_x[0] = part_out[0]
-    finish(near_steps)
-    near_sent += [near_over(2)]
-    next(far_steps)
-    far_sent += [far_over(1), far_over(NX - 1)]
-    for copy in part_sent:
-        copy.wait_recv()
-    part_y[0] = jnp.sum(part_x[...].astype(F32), axis=0).astype(BF16)
-    over_y = [send(part_y.at[0], part_y.at[NY - d], along_y(d)) for d in range(1, NY)]
+    straight += [send(mig_out.at[1], mig_in.at[1], along_z(half // PLANE))]
+    next(mig_steps)
     add_base(3)
     add_base(NY - 3)
+    for copy in part_sent:
+        copy.wait_recv()
+    part_y[0] = jnp.sum(part_x[...].astype(F32), axis=0).astype(BF16)
+    over_y = [send(part_y.at[0], part_y.at[NY - d], along_y(d)) for d in (4, 3, 5, 2, 6, 1, 7)]
+    for copy in far_sent:
+        copy.wait_recv()
+    expand_over += [expands_over(far)]
+    next(mig_steps)
     next(y_steps)
     add_base(4)
-    finish(far_steps)
-    far_sent += [far_over(2)]
-    next(mig_steps)
-    next(mig_steps)
     next(mig_steps)
     from_z = (2 * NZ - z_offset - carry) % NZ
     arrived_ref[2] = mig_z[from_z]
     for k, copy in enumerate(straight):
         copy.wait_recv()
         arrived_ref[k] = mig_in[k]
-    for copy in near_sent + far_sent:
-        copy.wait_recv()
-    expands = []
-    for b in range(BLOCKS):
-        oz, ow = stored[b] // PLANE, stored[b] % PLANE
-        at = (ow // NC - x + NX) % NX * NC + (ow % NC - c + NC) % NC
-        expands.append(expand_x[at, pick(EXPAND_AT, (oz - z + NZ) % NZ)])
+    for copy in expand_over:
+        copy.wait_recv()
+    expands = [
+        expand_x[plane_slot(stored[b] % PLANE), pick(ADAPTER_AT, (stored[b] // PLANE - z + NZ) % NZ)]
+        for b in range(BLOCKS)
+    ]
+    for copy in copies:
+        if not any(copy is one for one in over_y):
+            copy.wait_send()
     for copy in over_y:
         copy.wait_recv()
     shrink = jnp.sum(part_y[...].astype(F32), axis=0).astype(BF16)
@@ -351,7 +337,7 @@
         deltas[k], deltas[k + 2] = out[:rows], out[rows:]
     fresh_ref[...] = (base + jnp.concatenate(deltas, axis=0)).astype(BF16)
 
-    for copy in copies:
+    for copy in over_y:
         copy.wait_send()
 
 
@@ -464,12 +450,11 @@
             pltpu.SemaphoreType.DMA((10,)),
             pltpu.VMEM((ROWS, PART), F32),
             pltpu.VMEM((NY, ROWS, PART), BF16),
-            pltpu.VMEM((PLANE, ROWS, PART + HD), BF16),
-            pltpu.VMEM((NZ, RANK, PART), BF16),
+            pltpu.VMEM((PLANE, ROWS + 16, WIDE), BF16),
+            pltpu.VMEM((NZ, RANK, WIDE), BF16),
             pltpu.VMEM((PLANE, NZ, RANK, HD), BF16),
             pltpu.VMEM((2, MIG_ROWS, HD), BF16),
             pltpu.VMEM((2, MIG_ROWS, HD), BF16),
-            pltpu.VMEM((PLANE, MIG_ROWS, HD), BF16),
             pltpu.VMEM((NZ, MIG_ROWS, HD), BF16),
             pltpu.VMEM((PLANE * ROWS, HD), F32),
             pltpu.VMEM((PLANE, HALF, HD), BF16),

time: 54.6 us -> 45.7 us (0.84)
  the two profiles are of different devices: /device:TPU:4 before, /device:TPU:1 now
where the time goes in v4:
time: 45.7 us; the launch traced here: 45.6 us
  Pallas kernels  44.8 us (98%)
  between operations  0.72 us (2%)
    pallas_call x1, Pallas kernels, body(): pl.pallas_call(comm_kernel, out_shape=(jax.ShapeDtypeStruct((ROWS, HD), B...  42.6 us
    pallas_call x1, Pallas kernels, body(): pl.pallas_call(attend_kernel, out_shape=(jax.ShapeDtypeStruct(queries.sha...  2.26 us

profile of v4, /device:TPU:1, one launch (start us, length us, event | category | flops | bytes accessed | tf_op | source)
XLA Modules:
  0.0 45.6 jit_solution(15130268724374932088)
XLA Ops:
  0.6 0.0 copy-start.4
  0.6 0.0 copy-start.1
  0.7 0.0 copy-start
  0.7 0.0 copy-start.3
  0.7 0.0 copy-start.2
  0.7 42.6 %gather_and_project.1 = (bf16[64,128]{1,0:T(8,128)(2,1)S(1)}, bf16[3,144,128]{2,1,0:T(8,128)(2,1)S(1)}) custom-call(bf16[16,4,1024]{2,1,0:T(4,128)(2,1)} %tok_hbm.1, bf16[8192,128]{1,0:T(8,128)(2,1)} %w_hbm.1, bf16[16,64,128]{2,1,0:T(8,128)(2,1)} %keys_ref.1, bf16[16,64,128]{2,1,0:T(8,128)(2,1)} %values_ref.1, s32[16]{0:T(128)} %length_ref.1, ...), custom_call_target="tpu_custom_call" | custom-call | tf_op jit(solution)/shard_map/gather_and_project/pallas_call | solution.py:433
  43.3 0.0 copy-done.4
  43.3 0.0 copy-done.1
  43.3 0.0 copy-done
  43.3 0.0 copy-done.3
  43.3 0.0 copy-done.2
  43.3 2.3 %place_and_attend.1 = (bf16[16,4,1024]{2,1,0:T(4,128)(2,1)}, bf16[16,64,128]{2,1,0:T(8,128)(2,1)}, bf16[16,64,128]{2,1,0:T(8,128)(2,1)}) custom-call(bf16[16,4,1024]{2,1,0:T(4,128)(2,1)S(1)} %copy-done.2, bf16[16,4,128]{2,1,0:T(4,128)(2,1)S(1)} %copy-done.3, bf16[16,64,128]{2,1,0:T(8,128)(2,1)S(1)} %copy-done, bf16[16,64,128]{2,1,0:T(8,128)(2,1)S(1)} %copy-done.1, ...), custom_call_target="tpu_custom_call" | custom-call | tf_op jit(solution)/shard_map/place_and_attend/pallas_call | solution.py:487
Async XLA Ops:
  0.6 42.6 %copy-start.4 = (s32[16]{0:T(128)S(1)}, s32[16]{0:T(128)}, u32[]{:S(2)}) copy-start(s32[16]{0:T(128)} %length_ref.1) | copy-start | bytes 196
  0.6 42.6 %copy-start.1 = (bf16[16,64,128]{2,1,0:T(8,128)(2,1)S(1)}, bf16[16,64,128]{2,1,0:T(8,128)(2,1)}, u32[]{:S(2)}) copy-start(bf16[16,64,128]{2,1,0:T(8,128)(2,1)} %values_ref.1) | copy-start | bytes 786436
  0.7 42.6 %copy-start = (bf16[16,64,128]{2,1,0:T(8,128)(2,1)S(1)}, bf16[16,64,128]{2,1,0:T(8,128)(2,1)}, u32[]{:S(2)}) copy-start(bf16[16,64,128]{2,1,0:T(8,128)(2,1)} %keys_ref.1) | copy-start | bytes 786436
  0.7 42.6 %copy-start.3 = (bf16[16,4,128]{2,1,0:T(4,128)(2,1)S(1)}, bf16[16,4,128]{2,1,0:T(4,128)(2,1)}, u32[]{:S(2)}) copy-start(bf16[16,4,128]{2,1,0:T(4,128)(2,1)} %draft_ref.1) | copy-start | bytes 49156
  0.7 42.6 %copy-start.2 = (bf16[16,4,1024]{2,1,0:T(4,128)(2,1)S(1)}, bf16[16,4,1024]{2,1,0:T(4,128)(2,1)}, u32[]{:S(2)}) copy-start(bf16[16,4,1024]{2,1,0:T(4,128)(2,1)} %q_ref.1) | copy-start | bytes 393220

commit v5 on v4

--- a/solution.py
+++ b/solution.py
@@ -41,10 +41,63 @@
     return lax.broadcasted_iota(jnp.int32, shape, len(shape) - 1)
 
 
+class Placed:
+    def __init__(self, arrived_ref, length_ref):
+        self.arrived_ref = arrived_ref
+        notes = [arrived_ref[a, 2 * CACHE :].astype(F32) for a in range(3)]
+        self.landing = [rows[0:1] for rows in notes]
+        self.filled = []
+        for s in range(SLOTS):
+            fill = jnp.full((1, HD), length_ref[s].astype(F32))
+            for a in range(3):
+                fill = jnp.where(self.landing[a] == float(s), notes[a][1:2], fill)
+            self.filled.append(fill)
+
+    def fill(self, old_ref, first_row, new, out_ref):
+        spot = lax.broadcasted_iota(jnp.int32, (CACHE, HD), 0).astype(F32)
+        for s in range(SLOTS):
+            held = old_ref[s].astype(F32)
+            for a in range(3):
+                came = self.arrived_ref[a, first_row : first_row + CACHE].astype(F32)
+                held = jnp.where(self.landing[a] == float(s), came, held)
+            after = spot - self.filled[s]
+            rows = new(s)
+            for j in range(STEPS):
+                held = jnp.where(after == float(j), rows[j : j + 1], held)
+            out_ref[s] = held.astype(BF16)
+
+
+def scores_and_weights(placed, q_ref, keys_ref, weights_ref):
+    group = q_ref.shape[2] // HD
+    heads = group * STEPS
+    lane = lanes((1, HD))
+    row_at = lax.broadcasted_iota(jnp.int32, (2 * heads, HD), 0)
+    lane_at = lanes((2 * heads, HD))
+    same = (row_at // heads) == (lane_at // CACHE)
+    ahead = (lane_at % CACHE - row_at % STEPS).astype(F32)
+    scale = 1.0 / math.sqrt(HD)
+    scores = []
+    for pair in range(SLOTS // 2):
+        queries = []
+        for s in (2 * pair, 2 * pair + 1):
+            query = q_ref[s].astype(F32)
+            queries += [query[:, g * HD : (g + 1) * HD] for g in range(group)]
+        stacked = jnp.concatenate(queries, axis=0).astype(BF16)
+        both = keys_ref[2 * pair : 2 * pair + 2].reshape(2 * CACHE, HD)
+        scores.append(lax.dot_general(stacked, both, (((1,), (1,)), ((), ())), preferred_element_type=F32) * scale)
+    for pair, score in enumerate(scores):
+        allowed = same & (ahead <= jnp.where(lane < CACHE, placed.filled[2 * pair], placed.filled[2 * pair + 1]))
+        masked = jnp.where(allowed, score, -1e30)
+        top = jnp.max(masked, axis=-1, keepdims=True)
+        raised = jnp.where(allowed, jnp.exp(masked - top), 0.0)
+        weights_ref[pair] = (raised / jnp.sum(raised, axis=-1, keepdims=True)).astype(BF16)
+
+
 def comm_kernel(
     tok_hbm, w_hbm, keys_hbm, values_hbm, length_hbm, mig_hbm, index_hbm, owner_hbm, shrink_hbm, expand_hbm,
-    fresh_ref, arrived_ref,
-    tok_ref, w_ref, keys_ref, values_ref, length_ref, mig_ref, index_ref, owner_ref, load_sem, tok_f32,
+    q_hbm, draft_hbm,
+    fresh_ref, arrived_ref, ko_ref, weights_ref,
+    q_ref, draft_ref, tok_ref, w_ref, keys_ref, values_ref, length_ref, mig_ref, index_ref, owner_ref, load_sem, tok_f32,
     tok_y, tok_x, adapter_z, expand_x, mig_out, mig_in, mig_z,
     acc, part_out, part_x, part_y, send_sem, recv_sem,
 ):
@@ -76,8 +129,6 @@
 
     def plane_at(dx, dc):
         return dc * NX + X_AT[dx % NX]
-
-    far_first = [(dx, dc) for dx in (2, 1, 3, 0) for dc in range(NC) if dx or dc]
 
     loads = [
         pltpu.make_async_copy(src, dst, load_sem.at[k])
@@ -92,17 +143,16 @@
             (keys_hbm, keys_ref),
             (values_hbm, values_ref),
             (w_hbm, w_ref),
+            (q_hbm, q_ref),
+            (draft_hbm, draft_ref),
         ])
     ]
-    load_w = loads.pop()
+    late_loads = [loads.pop() for _ in range(3)]
     for load in loads:
         load.start()
 
     barrier = pltpu.get_barrier_semaphore()
-    others = [along_z(d) for d in (1, -1, 2, -2, NZ // 2)]
-    others += [along_y(d) for d in range(1, NY)]
-    others += [in_plane(dx, dc) for dx, dc in far_first]
-    others += [((r + 1) % REPLICAS, t), ((r + REPLICAS - 1) % REPLICAS, t)]
+    others = [along_z(1), along_z(-1), along_y(1), along_y(-1), in_plane(1, 0), in_plane(-1, 0), sibling]
     for other in others:
         pl.semaphore_signal(barrier, inc=1, device_id=other, device_id_type=MESH)
 
@@ -158,9 +208,6 @@
         [lambda d: mig_z.at[d, pl.ds(0, CACHE)], lambda d: mig_z.at[d, pl.ds(CACHE, MIG_ROWS - CACHE)]],
     )
 
-    def to_plane(src, dst):
-        return [send(src(plane_at(dx, dc)), dst(plane_at(-dx, dc)), in_plane(dx, dc)) for dx, dc in far_first]
-
     def expands_along_x(some):
         return [
             send(expand_x.at[0, some], expand_x.at[plane_at(-dx, 0), some], in_plane(dx, 0)) for dx in (2, 1, 3)
@@ -220,11 +267,12 @@
     next(x_steps)
     tok_y[0] = own
     next(y_steps)
-    load_w.start()
+    for load in late_loads:
+        load.start()
     for which in range(2):
         mig_out[which] = leaving(which)
-    straight = [send(mig_out.at[0], mig_in.at[0], ((r + 1) % REPLICAS, t))]
-    load_w.wait()
+    for load in late_loads:
+        load.wait()
     add_base(0)
     next(z_steps)
     next(x_steps)
@@ -285,27 +333,42 @@
     acc[...] = add_products(2, 1)
     next(z_steps)
 
-    total = add_products(3, 1).reshape(PLANE, ROWS, HD)
-    total = total + jnp.concatenate([total[:, :, RANK:], total[:, :, :RANK]], axis=-1)
-    total = jnp.where(lanes((PLANE, HALF, HD)) < RANK, total[:, :HALF], total[:, HALF:])
-    part_out[...] = total.astype(BF16)
-    part_sent = to_plane(lambda at: part_out.at[at], lambda at: part_x.at[at])
+    some = adapter_z[NZ - 2 : NZ, :, 0:PART].reshape(2 * RANK, PART)
+    nearer, farther = (((r + d * PLANE) % REPLICAS).astype(F32) for d in (5, 4))
+    wanted = jnp.where(lane < RANK, nearer, farther)
+    part_sent = []
+    for dx in (2, 1, 3, 0):
+        slots = [plane_at(dx, dc) for dc in range(NC)]
+        product = lax.dot_general(
+            jnp.concatenate([tok_x[at, 0:ROWS, 0:PART] for at in slots], axis=0), some, (((1,), (1,)), ((), ())),
+            preferred_element_type=F32,
+        )
+        for dc, at in enumerate(slots):
+            mine = tok_x[at, 0:ROWS, PART:].astype(F32) == wanted
+            total = acc[at * ROWS : (at + 1) * ROWS] + jnp.where(mine, product[dc * ROWS : (dc + 1) * ROWS], 0.0)
+            total = total + jnp.concatenate([total[:, RANK:], total[:, :RANK]], axis=-1)
+            total = jnp.where(lanes((HALF, HD)) < RANK, total[:HALF], total[HALF:]).astype(BF16)
+            if dx or dc:
+                part_out[at] = total
+                part_sent.append(send(part_out.at[at], part_x.at[plane_at(-dx, dc)], in_plane(dx, dc)))
+            else:
+                part_x[0] = total
     expand_x[0, NEAR:] = adapter_z[NEAR:, :, PART:]
     far_sent = expands_along_x(far)
-    part_x[0] = part_out[0]
-    straight += [send(mig_out.at[1], mig_in.at[1], along_z(half // PLANE))]
+    straight = [None, send(mig_out.at[1], mig_in.at[1], along_z(half // PLANE))]
     next(mig_steps)
+    straight[0] = send(mig_out.at[0], mig_in.at[0], ((r + 1) % REPLICAS, t))
     add_base(3)
     add_base(NY - 3)
     for copy in part_sent:
         copy.wait_recv()
+    next(y_steps)
     part_y[0] = jnp.sum(part_x[...].astype(F32), axis=0).astype(BF16)
     over_y = [send(part_y.at[0], part_y.at[NY - d], along_y(d)) for d in (4, 3, 5, 2, 6, 1, 7)]
     for copy in far_sent:
         copy.wait_recv()
     expand_over += [expands_over(far)]
     next(mig_steps)
-    next(y_steps)
     add_base(4)
     next(mig_steps)
     from_z = (2 * NZ - z_offset - carry) % NZ
@@ -313,6 +376,9 @@
     for k, copy in enumerate(straight):
         copy.wait_recv()
         arrived_ref[k] = mig_in[k]
+    placed = Placed(arrived_ref, length_ref)
+    placed.fill(keys_ref, 0, lambda s: draft_ref[s].astype(F32), ko_ref)
+    scores_and_weights(placed, q_ref, ko_ref, weights_ref)
     for copy in expand_over:
         copy.wait_recv()
     expands = [
@@ -342,66 +408,22 @@
 
 
 def attend_kernel(
-    q_ref, draft_ref, keys_ref, values_ref, length_ref, arrived_ref, fresh_ref,
-    out_hbm, ko_hbm, vo_hbm, out_ref, ko_ref, vo_ref, sem,
+    keys_ref, weights_ref, values_ref, length_ref, arrived_ref, fresh_ref,
+    out_hbm, ko_hbm, vo_hbm, out_ref, vo_ref, sem,
 ):
-    group = q_ref.shape[2] // HD
+    keys_gone = pltpu.make_async_copy(keys_ref, ko_hbm, sem.at[0])
+    keys_gone.start()
+    group = out_ref.shape[2] // HD
     heads = group * STEPS
-    spot = lax.broadcasted_iota(jnp.int32, (CACHE, HD), 0).astype(F32)
-    landing = [arrived_ref[a, 2 * CACHE : 2 * CACHE + 1, :].astype(F32) for a in range(3)]
-    lengths = [arrived_ref[a, 2 * CACHE + 1 : 2 * CACHE + 2, :].astype(F32) for a in range(3)]
-    lane = lanes((1, HD))
-    row_at = lax.broadcasted_iota(jnp.int32, (2 * heads, HD), 0)
-    lane_at = lanes((2 * heads, HD))
-    same = (row_at // heads) == (lane_at // CACHE)
-    ahead = (lane_at % CACHE - row_at % STEPS).astype(F32)
-    scale = 1.0 / math.sqrt(HD)
-    pairs = range(SLOTS // 2)
-
-    filled = []
-    for s in range(SLOTS):
-        fill = jnp.full((1, HD), length_ref[s].astype(F32))
-        for a in range(3):
-            fill = jnp.where(landing[a] == float(s), lengths[a], fill)
-        filled.append(fill)
-
-    def place(old_ref, first_row, new, out):
-        for s in range(SLOTS):
-            held = old_ref[s].astype(F32)
-            for a in range(3):
-                came = arrived_ref[a, first_row : first_row + CACHE].astype(F32)
-                held = jnp.where(landing[a] == float(s), came, held)
-            after = spot - filled[s]
-            rows = new(s)
-            for j in range(STEPS):
-                held = jnp.where(after == float(j), rows[j : j + 1], held)
-            out[s] = held.astype(BF16)
-
-    place(keys_ref, 0, lambda s: draft_ref[s].astype(F32), ko_ref)
-    keys_gone = pltpu.make_async_copy(ko_ref, ko_hbm, sem.at[0])
-    keys_gone.start()
-    scores = []
-    for pair in pairs:
-        queries = []
-        for s in (2 * pair, 2 * pair + 1):
-            query = q_ref[s].astype(F32)
-            queries += [query[:, g * HD : (g + 1) * HD] for g in range(group)]
-        stacked = jnp.concatenate(queries, axis=0).astype(BF16)
-        both = ko_ref[2 * pair : 2 * pair + 2].reshape(2 * CACHE, HD)
-        scores.append(lax.dot_general(stacked, both, (((1,), (1,)), ((), ())), preferred_element_type=F32) * scale)
-    place(values_ref, CACHE, lambda s: fresh_ref[s * STEPS : (s + 1) * STEPS].astype(F32), vo_ref)
+    placed = Placed(arrived_ref, length_ref)
+    placed.fill(
+        values_ref, CACHE, lambda s: fresh_ref[s * STEPS : (s + 1) * STEPS].astype(F32), vo_ref
+    )
     values_gone = pltpu.make_async_copy(vo_ref, vo_hbm, sem.at[1])
     values_gone.start()
-    weights = []
-    for pair in pairs:
-        allowed = same & (ahead <= jnp.where(lane < CACHE, filled[2 * pair], filled[2 * pair + 1]))
-        masked = jnp.where(allowed, scores[pair], -1e30)
-        top = jnp.max(masked, axis=-1, keepdims=True)
-        raised = jnp.where(allowed, jnp.exp(masked - top), 0.0)
-        weights.append((raised / jnp.sum(raised, axis=-1, keepdims=True)).astype(BF16))
-    for pair in pairs:
+    for pair in range(SLOTS // 2):
         both = vo_ref[2 * pair : 2 * pair + 2].reshape(2 * CACHE, HD)
-        attended = jnp.dot(weights[pair], both, preferred_element_type=F32)
+        attended = jnp.dot(weights_ref[pair], both, preferred_element_type=F32)
         for k in range(2):
             for g in range(group):
                 at = k * heads + g * STEPS
@@ -430,15 +452,19 @@
     vmem = pl.BlockSpec(memory_space=pltpu.VMEM)
     hbm = pl.BlockSpec(memory_space=pltpu.HBM)
     smem = pl.BlockSpec(memory_space=pltpu.SMEM)
-    fresh, arrived = pl.pallas_call(
+    fresh, arrived, keys_out, weights = pl.pallas_call(
         comm_kernel,
         out_shape=(
             jax.ShapeDtypeStruct((ROWS, HD), BF16),
             jax.ShapeDtypeStruct((3, MIG_ROWS, HD), BF16),
+            jax.ShapeDtypeStruct(key_cache_before.shape, BF16),
+            jax.ShapeDtypeStruct((SLOTS // 2, 2 * queries.shape[2] // HD * STEPS, 2 * CACHE), BF16),
         ),
-        in_specs=[hbm] * 10,
-        out_specs=(vmem, vmem),
+        in_specs=[hbm] * 12,
+        out_specs=(vmem, vmem, vmem, vmem),
         scratch_shapes=[
+            pltpu.VMEM(queries.shape, BF16),
+            pltpu.VMEM(draft_keys.shape, BF16),
             pltpu.VMEM(tokens.shape, BF16),
             pltpu.VMEM(value_matrix.shape, BF16),
             pltpu.VMEM(key_cache_before.shape, BF16),
@@ -447,7 +473,7 @@
             pltpu.SMEM((3, 1, 3), jnp.int32),
             pltpu.SMEM(block_adapter_index.shape, jnp.int32),
             pltpu.SMEM(adapter_replica.shape, jnp.int32),
-            pltpu.SemaphoreType.DMA((10,)),
+            pltpu.SemaphoreType.DMA((12,)),
             pltpu.VMEM((ROWS, PART), F32),
             pltpu.VMEM((NY, ROWS, PART), BF16),
             pltpu.VMEM((PLANE, ROWS + 16, WIDE), BF16),
@@ -481,6 +507,8 @@
                 adapter_replica,
                 jnp.swapaxes(adapter_shrink[0], 0, 1),
                 adapter_expand,
+                queries,
+                draft_keys,
             )
         )
     )
@@ -491,17 +519,16 @@
             jax.ShapeDtypeStruct(key_cache_before.shape, BF16),
             jax.ShapeDtypeStruct(value_cache_before.shape, BF16),
         ),
-        in_specs=[vmem, vmem, vmem, vmem, smem, vmem, vmem],
+        in_specs=[vmem, vmem, vmem, smem, vmem, vmem],
         out_specs=(hbm, hbm, hbm),
         scratch_shapes=[
             pltpu.VMEM(queries.shape, BF16),
-            pltpu.VMEM(key_cache_before.shape, BF16),
             pltpu.VMEM(value_cache_before.shape, BF16),
             pltpu.SemaphoreType.DMA((3,)),
         ],
         compiler_params=pltpu.CompilerParams(vmem_limit_bytes=24 * 1024 * 1024),
         name="place_and_attend",
-    )(queries, draft_keys, key_cache_before, value_cache_before, cache_length, arrived, fresh)
+    )(keys_out, weights, value_cache_before, cache_length, arrived, fresh)
 
 
 def solution(mesh):

time: 45.7 us -> 44.7 us (0.978)
  Pallas kernels: 44.8 us -> 43.8 us
    pallas_call x1, Pallas kernels: 2.26 us -> 1.74 us  [body(): pl.pallas_call(attend_kernel, out_shape=(jax.ShapeDtypeStruct(queries.sha...]
    pallas_call x1, Pallas kernels: 42.6 us -> 42.1 us  [body(): pl.pallas_call(comm_kernel, out_shape=(jax.ShapeDtypeStruct((ROWS, HD), B...]
where the time goes in v5:
time: 44.7 us; the launch traced here: 44.5 us
  Pallas kernels  43.8 us (98%)
  between operations  0.67 us (1%)
    pallas_call x1, Pallas kernels, body(): pl.pallas_call(comm_kernel, out_shape=(jax.ShapeDtypeStruct((ROWS, HD), B...  42.1 us
    pallas_call x1, Pallas kernels, body(): pl.pallas_call(attend_kernel, out_shape=(jax.ShapeDtypeStruct(queries.sha...  1.74 us

profile of v5, /device:TPU:1, one launch (start us, length us, event | category | flops | bytes accessed | tf_op | source)
XLA Modules:
  0.0 44.5 jit_solution(5256853910668242384)
XLA Ops:
  0.6 0.0 copy-start.1
  0.6 0.0 copy-start
  0.7 42.1 %gather_and_project.1 = (bf16[64,128]{1,0:T(8,128)(2,1)S(1)}, bf16[3,144,128]{2,1,0:T(8,128)(2,1)S(1)}, bf16[16,64,128]{2,1,0:T(8,128)(2,1)S(1)}, bf16[8,64,128]{2,1,0:T(8,128)(2,1)S(1)}) custom-call(bf16[16,4,1024]{2,1,0:T(4,128)(2,1)} %tok_hbm.1, bf16[8192,128]{1,0:T(8,128)(2,1)} %w_hbm.1, bf16[16,64,128]{2,1,0:T(8,128)(2,1)} %keys_hbm.1, ...), custom_call_target="tpu_custom_call" | custom-call | tf_op jit(solution)/shard_map/gather_and_project/pallas_call | solution.py:455
  42.8 0.0 copy-done.1
  42.8 0.0 copy-done
  42.8 1.7 %place_and_attend.1 = (bf16[16,4,1024]{2,1,0:T(4,128)(2,1)}, bf16[16,64,128]{2,1,0:T(8,128)(2,1)}, bf16[16,64,128]{2,1,0:T(8,128)(2,1)}) custom-call(bf16[16,64,128]{2,1,0:T(8,128)(2,1)S(1)} %get-tuple-element.7.keys_ref, bf16[8,64,128]{2,1,0:T(8,128)(2,1)S(1)} %get-tuple-element.8.weights_ref, bf16[16,64,128]{2,1,0:T(8,128)(2,1)S(1)} %copy-done, ...), custom_call_target="tpu_custom_call" | custom-call | tf_op jit(solution)/shard_map/place_and_attend/pallas_call | solution.py:515
Async XLA Ops:
  0.6 42.1 %copy-start.1 = (s32[16]{0:T(128)S(1)}, s32[16]{0:T(128)}, u32[]{:S(2)}) copy-start(s32[16]{0:T(128)} %length_ref.1) | copy-start | bytes 196
  0.6 42.1 %copy-start = (bf16[16,64,128]{2,1,0:T(8,128)(2,1)S(1)}, bf16[16,64,128]{2,1,0:T(8,128)(2,1)}, u32[]{:S(2)}) copy-start(bf16[16,64,128]{2,1,0:T(8,128)(2,1)} %values_ref.1) | copy-start | bytes 786436

commit v6 on v5

--- a/solution.py
+++ b/solution.py
@@ -130,6 +130,14 @@
     def plane_at(dx, dc):
         return dc * NX + X_AT[dx % NX]
 
+    settled = 0
+
+    def settle(count):
+        nonlocal settled
+        for copy in copies[settled:count]:
+            copy.wait_send()
+        settled = max(settled, count)
+
     loads = [
         pltpu.make_async_copy(src, dst, load_sem.at[k])
         for k, (src, dst) in enumerate([
@@ -280,6 +288,7 @@
     next(y_steps)
     add_base(1)
     add_base(NY - 1)
+    before_3 = len(copies)
     next(z_steps)
     next(x_steps)
     tokens_over += [send(tok_x.at[3], tok_x.at[NX + 3], sibling)]
@@ -331,6 +340,8 @@
     add_base(2)
     add_base(NY - 2)
     acc[...] = add_products(2, 1)
+    before_last = len(copies)
+    settle(before_3)
     next(z_steps)
 
     some = adapter_z[NZ - 2 : NZ, :, 0:PART].reshape(2 * RANK, PART)
@@ -358,17 +369,19 @@
     straight = [None, send(mig_out.at[1], mig_in.at[1], along_z(half // PLANE))]
     next(mig_steps)
     straight[0] = send(mig_out.at[0], mig_in.at[0], ((r + 1) % REPLICAS, t))
+    settle(before_last)
+    for copy in part_sent:
+        copy.wait_recv()
+    next(y_steps)
+    part_y[0] = jnp.sum(part_x[...].astype(F32), axis=0).astype(BF16)
+    before_y = len(copies)
+    over_y = [send(part_y.at[0], part_y.at[NY - d], along_y(d)) for d in (4, 3, 5, 2, 6, 1, 7)]
+    for copy in far_sent:
+        copy.wait_recv()
+    expand_over += [expands_over(far)]
+    next(mig_steps)
     add_base(3)
     add_base(NY - 3)
-    for copy in part_sent:
-        copy.wait_recv()
-    next(y_steps)
-    part_y[0] = jnp.sum(part_x[...].astype(F32), axis=0).astype(BF16)
-    over_y = [send(part_y.at[0], part_y.at[NY - d], along_y(d)) for d in (4, 3, 5, 2, 6, 1, 7)]
-    for copy in far_sent:
-        copy.wait_recv()
-    expand_over += [expands_over(far)]
-    next(mig_steps)
     add_base(4)
     next(mig_steps)
     from_z = (2 * NZ - z_offset - carry) % NZ
@@ -385,9 +398,7 @@
         expand_x[plane_slot(stored[b] % PLANE), pick(ADAPTER_AT, (stored[b] // PLANE - z + NZ) % NZ)]
         for b in range(BLOCKS)
     ]
-    for copy in copies:
-        if not any(copy is one for one in over_y):
-            copy.wait_send()
+    settle(before_y)
     for copy in over_y:
         copy.wait_recv()
     shrink = jnp.sum(part_y[...].astype(F32), axis=0).astype(BF16)
@@ -403,8 +414,7 @@
         deltas[k], deltas[k + 2] = out[:rows], out[rows:]
     fresh_ref[...] = (base + jnp.concatenate(deltas, axis=0)).astype(BF16)
 
-    for copy in over_y:
-        copy.wait_send()
+    settle(len(copies))
 
 
 def attend_kernel(

time: 44.7 us -> 44.8 us (level)
  no operation moved by 1% of the time
where the time goes in v6:
time: 44.8 us; the launch traced here: 44.6 us
  Pallas kernels  43.9 us (98%)
  between operations  0.67 us (1%)
    pallas_call x1, Pallas kernels, body(): pl.pallas_call(comm_kernel, out_shape=(jax.ShapeDtypeStruct((ROWS, HD), B...  42.1 us
    pallas_call x1, Pallas kernels, body(): pl.pallas_call(attend_kernel, out_shape=(jax.ShapeDtypeStruct(queries.sha...  1.74 us

profile of v6, /device:TPU:1, one launch (start us, length us, event | category | flops | bytes accessed | tf_op | source)
XLA Modules:
  0.0 44.6 jit_solution(8521845948110521018)
XLA Ops:
  0.6 0.0 copy-start.1
  0.6 0.0 copy-start
  0.7 42.1 %gather_and_project.1 = (bf16[64,128]{1,0:T(8,128)(2,1)S(1)}, bf16[3,144,128]{2,1,0:T(8,128)(2,1)S(1)}, bf16[16,64,128]{2,1,0:T(8,128)(2,1)S(1)}, bf16[8,64,128]{2,1,0:T(8,128)(2,1)S(1)}) custom-call(bf16[16,4,1024]{2,1,0:T(4,128)(2,1)} %tok_hbm.1, bf16[8192,128]{1,0:T(8,128)(2,1)} %w_hbm.1, bf16[16,64,128]{2,1,0:T(8,128)(2,1)} %keys_hbm.1, ...), custom_call_target="tpu_custom_call" | custom-call | tf_op jit(solution)/shard_map/gather_and_project/pallas_call | solution.py:465
  42.8 0.0 copy-done.1
  42.8 0.0 copy-done
  42.8 1.7 %place_and_attend.1 = (bf16[16,4,1024]{2,1,0:T(4,128)(2,1)}, bf16[16,64,128]{2,1,0:T(8,128)(2,1)}, bf16[16,64,128]{2,1,0:T(8,128)(2,1)}) custom-call(bf16[16,64,128]{2,1,0:T(8,128)(2,1)S(1)} %get-tuple-element.7.keys_ref, bf16[8,64,128]{2,1,0:T(8,128)(2,1)S(1)} %get-tuple-element.8.weights_ref, bf16[16,64,128]{2,1,0:T(8,128)(2,1)S(1)} %copy-done, ...), custom_call_target="tpu_custom_call" | custom-call | tf_op jit(solution)/shard_map/place_and_attend/pallas_call | solution.py:525
Async XLA Ops:
  0.6 42.2 %copy-start.1 = (s32[16]{0:T(128)S(1)}, s32[16]{0:T(128)}, u32[]{:S(2)}) copy-start(s32[16]{0:T(128)} %length_ref.1) | copy-start | bytes 196
  0.6 42.2 %copy-start = (bf16[16,64,128]{2,1,0:T(8,128)(2,1)S(1)}, bf16[16,64,128]{2,1,0:T(8,128)(2,1)}, u32[]{:S(2)}) copy-start(bf16[16,64,128]{2,1,0:T(8,128)(2,1)} %values_ref.1) | copy-start | bytes 786436
